TPU v7x, 32 devices: a whole 2x2x4 slice. The times are simulated.
32 devices in a mesh: frame: 16 (over z, x, core), quad: 2 (over y).
Axes of the slice: x: 2, y: 2, z: 4, core: 2. Of those that a mesh axis runs over, the one named last changes fastest.
Arguments:
- activations: bfloat16 [64, 32, 1280], P('frame', 'quad'), may hold values from -48 to 48
- cotangent: bfloat16 [64, 32, 1280], P('frame', 'quad'), may hold values from -6 to 6
- spatial_weights: bfloat16 [4, 1280, 640], replicated, may hold values from -2 to 2
- spatial_gain: float32 [1280], replicated, may hold values from 0.1 to 1.9
- motion_weights: bfloat16 [4, 1280, 640], P(None, 'quad'), may hold values from -2 to 2
- motion_gain: float32 [1280], replicated, may hold values from 0.1 to 1.9
Outputs:
- block_output: bfloat16 [64, 32, 1280], P('frame', 'quad')
- input_grad: bfloat16 [64, 32, 1280], P('frame', 'quad')
- weight_grad: float32 [4, 1280, 640], P(None, ('frame', 'quad'))
- gain_grad: float32 [1280], P(('frame', 'quad'))
All inputs are finite; a program needn't handle non-finite values.
Results may differ from a plain program's by a relative error of at most 0.03.
Values may be sent and summed in bfloat16 or wider, within the bound.
No kernel may reach another device: no remote copies, remote signals or barrier semaphores. Data moves between devices by JAX's collectives and lax.ppermute only.
A program may use at most 128 MiB of HBM per device.

v0:
```python
import functools
import math

import jax
import jax.numpy as jnp
from jax import lax
from jax.experimental import pallas as pl
from jax.experimental.pallas import tpu as pltpu
from jax.sharding import PartitionSpec as P

HEADS = 4
HEAD_DIM = 160
EPSILON = 1e-05
SCALE = HEAD_DIM ** (-0.5)
F32 = jnp.float32
BF16 = jnp.bfloat16


def log2(n):
    return int(n).bit_length() - 1


def dot(a, b):
    return jnp.dot(a, b, preferred_element_type=F32)


def dot_t(a, b):
    return lax.dot_general(a, b, (((1,), (1,)), ((), ())), preferred_element_type=F32)


def t_dot(a, b):
    return lax.dot_general(a, b, (((0,), (0,)), ((), ())), preferred_element_type=F32)


def normalize(values):
    average = jnp.mean(values, axis=-1, keepdims=True)
    centred = values - average
    inv_scale = lax.rsqrt(jnp.mean(centred * centred, axis=-1, keepdims=True) + EPSILON)
    return centred * inv_scale, inv_scale


def normalize_back(grad_rows, unit_rows, inv_scale, gain):
    scaled = grad_rows * gain
    first_mean = jnp.mean(scaled, axis=-1, keepdims=True)
    second_mean = jnp.mean(scaled * unit_rows, axis=-1, keepdims=True)
    return inv_scale * (scaled - first_mean - unit_rows * second_mean)


def iota(shape, dim):
    return lax.broadcasted_iota(jnp.int32, shape, dim)


def head_mask(dtype):
    lane = iota((1, HEADS * HEAD_DIM), 1)
    return [
        jnp.where((lane >= h * HEAD_DIM) & (lane < (h + 1) * HEAD_DIM), 1.0, 0.0).astype(dtype)
        for h in range(HEADS)
    ]


def stack_heads(rows):
    return jnp.concatenate([rows * mask for mask in head_mask(rows.dtype)], axis=0)


def fold_heads(stacked):
    rows = stacked.shape[0] // HEADS
    total = None
    for h, mask in enumerate(head_mask(F32)):
        piece = stacked[h * rows : (h + 1) * rows] * mask
        total = piece if total is None else total + piece
    return total


def probabilities(query_stack, keys, same):
    scores = dot_t(query_stack, keys) * SCALE
    if same is not None:
        scores = jnp.where(same, scores, -1e30)
    highest = jnp.max(scores, axis=-1, keepdims=True)
    expo = jnp.exp(scores - highest)
    return expo / jnp.sum(expo, axis=-1, keepdims=True)


def attend(query, keys, values, same):
    probs = probabilities(stack_heads(query), keys, same)
    return fold_heads(dot(probs.astype(BF16), values)).astype(BF16)


def attend_back(query, keys, values, grad, same, probs=None):
    query_stack = stack_heads(query)
    grad_stack = stack_heads(grad)
    if probs is None:
        probs = probabilities(query_stack, keys, same)
    grad_probs = dot_t(grad_stack, values)
    inner = jnp.sum(probs * grad_probs, axis=-1, keepdims=True)
    grad_scores = (probs * (grad_probs - inner) * SCALE).astype(BF16)
    grad_query = fold_heads(dot(grad_scores, keys)).astype(BF16)
    grad_key = t_dot(grad_scores, query_stack).astype(BF16)
    grad_value = t_dot(probs.astype(BF16), grad_stack).astype(BF16)
    return grad_query, grad_key, grad_value


def rows_to_sent(quad, nq, fr, pq, transposed):
    rows = nq * fr * pq
    out_dim = 1 if transposed else 0
    out = iota((rows, rows), out_dim)
    src = iota((rows, rows), 1 - out_dim)
    cell = out >> log2(nq * fr)
    other = (out >> log2(fr)) & (nq - 1)
    frame = out & (fr - 1)
    want = (((other - quad) & (nq - 1)) << log2(fr * pq)) + (frame << log2(pq)) + cell
    return jnp.where(want == src, 1.0, 0.0).astype(BF16)


def received_to_rows(quad, nq, nf, fr, transposed):
    rows = nq * nf * fr
    out_dim = 1 if transposed else 0
    out = iota((rows, rows), out_dim)
    src = iota((rows, rows), 1 - out_dim)
    step = out >> log2(nf * fr)
    device = (out >> log2(fr)) & (nf - 1)
    frame = out & (fr - 1)
    want = (device << log2(nq * fr)) + (((step + quad) & (nq - 1)) << log2(fr)) + frame
    return jnp.where(want == src, 1.0, 0.0).astype(BF16)


def own_lanes(values, quad, nq):
    width = values.shape[1] // nq
    picked = values[:, :width]
    for t in range(1, nq):
        picked = jnp.where(quad == t, values[:, t * width : (t + 1) * width], picked)
    return picked


def place_lanes(parts, quad, nq):
    placed = []
    for t in range(nq):
        piece = parts[t]
        for q in range(1, nq):
            piece = jnp.where(quad == q, parts[(t - q) % nq], piece)
        placed.append(piece)
    return jnp.concatenate(placed, axis=1)


def frame_groups(nq, fr, pq):
    size = max(1, min(fr, 128 // (nq * pq)))
    return [(start, size) for start in range(0, fr, size)]


def pick_group(rows, group, nq, fr, pq):
    start, size = group
    if size == fr:
        return rows
    cut = rows.reshape(nq, fr, pq, rows.shape[-1])[:, start : start + size]
    return cut.reshape(nq * size * pq, rows.shape[-1])


def join_groups(pieces, nq, fr, pq):
    if len(pieces) == 1:
        return pieces[0]
    size = fr // len(pieces)
    width = pieces[0].shape[-1]
    joined = jnp.concatenate([p.reshape(nq, size, pq, width) for p in pieces], axis=1)
    return joined.reshape(nq * fr * pq, width)


def same_frame(nq, size, pq):
    if size == 1:
        return None
    rows = nq * size * pq
    shape = (HEADS * rows, rows)
    left = (iota(shape, 0) >> log2(pq)) & (size - 1)
    right = (iota(shape, 1) >> log2(pq)) & (size - 1)
    return left == right


def row_of(ref):
    return ref[...].reshape(1, -1)


def flat(ref):
    value = ref[...]
    return value.reshape(-1, value.shape[-1])


def flat_wide(ref):
    value = ref[...].astype(F32)
    return value.reshape(-1, value.shape[-1])


def spread(rows, like):
    return rows.reshape(like.shape).astype(like.dtype)


def spatial_kernel(dims, *refs):
    nq, nf, fr, pq = dims
    quad, xs, refs = refs[0][0], refs[1 : 1 + nq], refs[1 + nq :]
    gain1, gain2, pos, weights, kept_out, send_out = refs
    width = HEADS * HEAD_DIM
    wide = jnp.concatenate([flat_wide(x) for x in xs], axis=0)
    unit, _ = normalize(wide)
    normed = (unit * row_of(gain1)).astype(BF16)
    query = dot(normed, weights[0]).astype(BF16)
    keys = dot(normed, weights[1]).astype(BF16)
    values = dot(normed, weights[2]).astype(BF16)
    for i, part in enumerate((query, keys, values)):
        kept_out[:, i * width : (i + 1) * width] = part
    pieces = []
    for group in frame_groups(nq, fr, pq):
        same = same_frame(nq, group[1], pq)
        cut = [pick_group(part, group, nq, fr, pq) for part in (query, keys, values)]
        pieces.append(attend(*cut, same))
    out = join_groups(pieces, nq, fr, pq)
    hidden = (wide + dot_t(out, weights[3])).astype(BF16)
    kept_out[:, 3 * width :] = hidden
    unit_two, _ = normalize(hidden.astype(F32))
    table = jnp.broadcast_to(pos[...][:, None, :], (fr, pq, pos.shape[-1]))
    table = table.reshape(fr * pq, pos.shape[-1])
    table = jnp.concatenate([table] * nq, axis=0)
    normed_two = own_lanes(unit_two * row_of(gain2) + table, quad, nq).astype(BF16)
    send_out[...] = spread(dot(rows_to_sent(quad, nq, fr, pq, False), normed_two), send_out)


def order_kernel(dims, cot, send_out):
    nq, nf, fr, pq = dims
    rows = flat(cot)
    width = rows.shape[1] // nq
    shape = (nq * fr * pq, fr * pq)
    out, src = iota(shape, 0), iota(shape, 1)
    want = ((out & (fr - 1)) << log2(pq)) + (out >> log2(nq * fr))
    part = (out >> log2(fr)) & (nq - 1)
    total = None
    for t in range(nq):
        pick = jnp.where((want == src) & (part == t), 1.0, 0.0).astype(BF16)
        piece = dot(pick, rows[:, t * width : (t + 1) * width])
        total = piece if total is None else total + piece
    send_out[...] = spread(total, send_out)


def split_kernel(dims, quad_ref, received, *outs):
    nq, nf, fr, pq = dims
    order = received_to_rows(quad_ref[0], nq, nf, fr, False)
    rows = dot(order, flat_wide(received).astype(BF16)).astype(BF16)
    tokens = nf * fr
    for s in range(nq):
        outs[s][...] = rows[s * tokens : (s + 1) * tokens]


def join(refs):
    return jnp.concatenate([ref[...] for ref in refs], axis=0)


def cotangent_kernel(dims, *refs):
    nq, nf, fr, pq = dims
    weights, own_out, *sends = refs[nq:]
    product = dot(join(refs[:nq]), weights[3])
    tokens = nf * fr
    own_out[...] = product[:tokens]
    for s, send in enumerate(sends):
        send[...] = product[(s + 1) * tokens : (s + 2) * tokens].astype(BF16)


def motion_kernel(dims, quad_ref, received, weights, own_out, *sends):
    nq, nf, fr, pq = dims
    order = received_to_rows(quad_ref[0], nq, nf, fr, False)
    rows = dot(order, flat_wide(received).astype(BF16)).astype(BF16)
    tokens = nf * fr
    for k in range(3):
        width = weights.shape[-1]
        lanes = slice(k * width, (k + 1) * width)
        product = dot(rows, weights[k])
        own_out[:, lanes] = product[:tokens]
        for s, send in enumerate(sends):
            send[:, lanes] = product[(s + 1) * tokens : (s + 2) * tokens].astype(BF16)


def cut_kernel(dims, geo, received, *refs):
    nq, nf, fr, pq = dims
    cots, (keep, swap) = refs[:nq], refs[nq:]
    order = received_to_rows(geo[0], nq, nf, fr, False)
    normed = dot(order, flat_wide(received).astype(BF16))
    for i, rows in enumerate((normed, join(cots).astype(F32))):
        half = rows.shape[1] // 2
        low, high = rows[:, :half], rows[:, half:]
        keep[i] = jnp.where(geo[1] == 0, low, high).astype(BF16)
        swap[i] = jnp.where(geo[1] == 0, high, low).astype(BF16)


def temporal_kernel(dims, *refs):
    nq, nf, fr, pq = dims
    qkv_own, qkv_in = refs[0], refs[1:nq]
    grad_own, grad_in = refs[nq], refs[nq + 1 : 2 * nq]
    out = refs[2 * nq]
    width = HEADS * HEAD_DIM
    total = qkv_own[...]
    for part in qkv_in:
        total = total + part[...].astype(F32)
    grad = grad_own[...].astype(F32)
    for part in grad_in:
        grad = grad + part[...].astype(F32)
    query, keys, values = [total[:, k * width : (k + 1) * width].astype(BF16) for k in range(3)]
    grad = grad.astype(BF16)
    probs = probabilities(stack_heads(query), keys, None)
    motion_out = fold_heads(dot(probs.astype(BF16), values)).astype(BF16)
    grads = attend_back(query, keys, values, grad, None, probs)
    for k, piece in enumerate(grads + (motion_out,)):
        out[:, k * width : (k + 1) * width] = piece


def part_of(terms, k):
    width = HEADS * HEAD_DIM
    return jnp.concatenate([t[:, k * width : (k + 1) * width] for t in terms], axis=0)


def back_kernel(dims, quad_ref, *refs):
    nq, nf, fr, pq = dims
    terms, (weights, out) = refs[:nq], refs[nq:]
    order = received_to_rows(quad_ref[0], nq, nf, fr, True)
    grad = None
    for k in range(3):
        product = dot_t(part_of(terms, k), weights[k])
        grad = product if grad is None else grad + product
    delta = dot_t(part_of(terms, 3), weights[3])
    for i, rows in enumerate((grad, delta)):
        rows = dot(order, rows.astype(BF16))
        out[:, i * nq * fr : (i + 1) * nq * fr, :] = rows.reshape(nf, nq * fr, -1).astype(BF16)


def weight_kernel(dims, geo, keep, swapped, weights, pos, gain2, *refs):
    nq, nf, fr, pq = dims
    terms, refs = refs[: 2 * nq], refs[2 * nq :]
    keep_a, send_a, outs_b, (first, second) = refs[0], refs[1], refs[2:-2], refs[-2:]
    _, stage, block, width = first.shape
    quad, core, mid, turn = [geo[i] for i in range(4)]
    normed = jnp.concatenate([keep[0], swapped[0]], axis=0)
    cot = jnp.concatenate([keep[1], swapped[1]], axis=0)
    rows = normed.shape[1]
    grad = None
    for k in range(4):
        right = part_of(terms, k)
        product = t_dot(normed if k < 3 else cot, right)
        blocks = second if k == 3 else first
        for x in range(2):
            for z in range(stage):
                j = x * stage + z
                blocks[x, z] = product[j * block : (j + 1) * block]
        if k < 3:
            back = dot_t(right, weights[k, pl.ds(pl.multiple_of(core * rows, 16), rows), :])
            grad = back if grad is None else grad + back
        if k < 2:
            for r in range(stage):
                z = (turn + r) & (stage - 1)
                keep_a[r, k] = blocks[mid, z].astype(BF16)
                send_a[r, k] = blocks[1 - mid, z].astype(BF16)

    def core_lanes(values):
        values = own_lanes(values, quad, nq)
        return jnp.where(core == 0, values[:, :rows], values[:, rows:])

    table = jnp.concatenate([core_lanes(pos[...])] * (2 * nq), axis=0)
    gain = jnp.sum(grad * (normed.astype(F32) - table), axis=0, keepdims=True)
    gain = gain / core_lanes(row_of(gain2))
    extra = jnp.concatenate([gain, jnp.zeros((1, width - rows), F32)], axis=1)
    extra = jnp.where(iota((8, width), 0) == 0, extra, 0.0)
    for r in range(stage):
        z = (turn + r) & (stage - 1)
        for x, at in enumerate((mid, 1 - mid)):
            rows_out = jnp.concatenate([first[at, z], second[at, z], extra], axis=0)
            outs_b[r][x] = rows_out.astype(BF16)


def pair_kernel(dims, keep, moved, *outs):
    for r, out in enumerate(outs):
        out[...] = (keep[r].astype(F32) + moved[r].astype(F32)).astype(BF16)


def add_kernel(dims, left, right, *outs):
    total = (left[...].astype(F32) + right[...].astype(F32)).astype(BF16)
    if len(outs) == 1:
        outs[0][...] = total
    else:
        for i, out in enumerate(outs):
            out[...] = total[i]


def middle_kernel(dims, *refs):
    nq, nf, fr, pq = dims
    quad, received, cots = refs[0][0], refs[1 : 1 + nq], refs[1 + nq : 1 + 2 * nq]
    kept, gain2, block_out, grad_out = refs[1 + 2 * nq :]
    own = fr * pq
    order = rows_to_sent(quad, nq, fr, pq, True)

    def lanes(i):
        parts = []
        for r in received:
            rows = r[:, i * nq * fr : (i + 1) * nq * fr, :].astype(F32)
            parts.append(dot(order, rows.reshape(nf * nq * fr, -1).astype(BF16)))
        return place_lanes(parts, quad, nq)

    hidden = kept[:, 3 * HEADS * HEAD_DIM :].astype(F32)
    grad_normed, delta = lanes(0), lanes(1)
    block_out[...] = spread(hidden[:own] + delta[:own], block_out)
    unit_two, inv_two = normalize(hidden)
    cot = jnp.concatenate([flat_wide(c) for c in cots], axis=0)
    back = normalize_back(grad_normed, unit_two, inv_two, row_of(gain2))
    grad_out[...] = (cot + back).astype(BF16)


def tail_kernel(dims, grad_hidden, xs, kept, gain1, weights, in_grad):
    nq, nf, fr, pq = dims
    own, width = fr * pq, HEADS * HEAD_DIM
    grad_out = dot(grad_hidden[...], weights[3]).astype(BF16)
    parts = [kept[:, i * width : (i + 1) * width] for i in range(3)] + [grad_out]
    pieces = []
    for group in frame_groups(nq, fr, pq):
        same = same_frame(nq, group[1], pq)
        pieces.append(attend_back(*[pick_group(p, group, nq, fr, pq) for p in parts], same))
    grads = [join_groups([p[i] for p in pieces], nq, fr, pq)[:own] for i in range(3)]
    grad_one = dot_t(grads[0], weights[0]) + dot_t(grads[1], weights[1]) + dot_t(grads[2], weights[2])
    unit_one, inv_one = normalize(flat_wide(xs))
    back = normalize_back(grad_one, unit_one, inv_one, row_of(gain1))
    in_grad[...] = spread(grad_hidden[...][:own].astype(F32) + back, in_grad)


def call(kernel, name, outs, args, vmem, micros, scratch=()):
    in_specs = []
    for arg in args:
        space = pltpu.SMEM if arg.dtype == jnp.int32 else pltpu.VMEM
        in_specs.append(pl.BlockSpec(memory_space=space))
    return list(
        pl.pallas_call(
            kernel,
            out_shape=outs,
            in_specs=in_specs,
            out_specs=[pl.BlockSpec(memory_space=pltpu.VMEM) for _ in outs],
            scratch_shapes=list(scratch),
            compiler_params=pltpu.CompilerParams(vmem_limit_bytes=vmem * 1024 * 1024),
            cost_estimate=pl.CostEstimate(
                flops=int(micros * 1e9), bytes_accessed=2**20, transcendentals=0
            ),
            name=name,
        )(*args)
    )


def after(value, *others):
    return lax.optimization_barrier((value,) + others)[0]


def sds(*shape, dtype=BF16):
    return jax.ShapeDtypeStruct(shape, dtype)


def positional(first, frames, channels):
    frame_pos = (first + lax.broadcasted_iota(jnp.int32, (frames, channels), 0)).astype(F32)
    lane = lax.broadcasted_iota(jnp.int32, (frames, channels), 1)
    freq_index = (lane >> 1).astype(F32)
    phases = frame_pos * jnp.exp(freq_index * (-2.0 * math.log(10000.0) / channels))
    return jnp.sin(phases + (lane & 1).astype(F32) * (0.5 * math.pi))


def local(nq, nf, activations, cotangent, spatial_weights, spatial_gain, motion_weights, motion_gain):
    fr, pq, channels = activations.shape
    dims = (nq, nf, fr, pq)
    width = spatial_weights.shape[-1]
    half = channels // nq
    rows = nq * fr * pq
    tokens = nf * fr
    small = 16 if rows <= 256 else 40
    big = 16 if rows <= 256 else 52
    quad = lax.axis_index("quad")
    frame = lax.axis_index("frame")


    def from_quad(x, s):
        return lax.ppermute(x, "quad", [((d + s) % nq, d) for d in range(nq)])

    def to_quad(x, s):
        return lax.ppermute(x, "quad", [(d, (d + s) % nq) for d in range(nq)])

    def swap(x):
        return lax.all_to_all(x, "frame", split_axis=0, concat_axis=0, tiled=True)

    def run(kernel, name, outs, args, micros, vmem=small, **options):
        kernel = functools.partial(kernel, dims)
        return call(kernel, name, outs, args, vmem, micros, **options)

    def move(x, pairs):
        return lax.ppermute(x, "frame", pairs)

    core, mid, turn = frame % 2, (frame // 2) % 2, frame // 4
    geo = jnp.stack([quad, core, mid, turn]).astype(jnp.int32)
    flip_core = [(g, g ^ 1) for g in range(nf)]
    flip_mid = [(g, g ^ 2) for g in range(nf)]
    ring = [(g, (g + 4) % nf) for g in range(nf)]

    gain1, gain2 = spatial_gain, motion_gain
    sent = sds(nf, nq * fr, half)
    acts = [activations] + [from_quad(activations, s) for s in range(1, nq)]
    (cot_send,) = run(order_kernel, "order_cotangent", [sent], [cotangent], 0.3)
    cot_recv = swap(cot_send)
    cot_later = after(cotangent, acts[-1])
    cots = [cotangent] + [from_quad(cot_later, s) for s in range(1, nq)]
    pos = positional(frame * fr, fr, channels)

    kept, send = run(
        spatial_kernel,
        "spatial_forward",
        [sds(rows, 3 * width + channels), sent],
        [geo] + acts + [gain1, gain2, pos, spatial_weights],
        3,
        big,
    )
    received = swap(send)

    cot_parts = run(
        split_kernel,
        "split_cotangent",
        [sds(tokens, half)] * nq,
        [geo, after(cot_recv, send)],
        0.3,
    )
    cot_parts = [cot_parts[0]] + [to_quad(cot_parts[nq - s], nq - s) for s in range(1, nq)]
    grad_parts = run(
        cotangent_kernel,
        "cotangent_projection",
        [sds(tokens, width, dtype=F32)] + [sds(tokens, width)] * (nq - 1),
        [after(cot_parts[0], cots[-1])] + cot_parts[1:] + [motion_weights],
        0.4,
    )
    grad_own = grad_parts[0]
    table = positional(after(frame * 0, cot_parts[0]), tokens, channels)
    grad_parts = [grad_own] + [to_quad(p, s + 1) for s, p in enumerate(grad_parts[1:])]

    qkv_parts = run(
        motion_kernel,
        "motion_projection",
        [sds(tokens, 3 * width, dtype=F32)] + [sds(tokens, 3 * width)] * (nq - 1),
        [geo, after(received, grad_own, table), motion_weights],
        0.8,
    )
    factors, factors_out = run(
        cut_kernel,
        "cut_factors",
        [sds(2, rows, half // 2)] * 2,
        [geo, after(received, qkv_parts[0])] + cot_parts,
        0.5,
    )
    qkv_parts = [qkv_parts[0]] + [to_quad(part, s + 1) for s, part in enumerate(qkv_parts[1:])]
    factors_in = move(factors_out, flip_core)

    (terms,) = run(
        temporal_kernel,
        "temporal_attention",
        [sds(tokens, 4 * width)],
        [after(qkv_parts[0], factors)] + qkv_parts[1:] + grad_parts,
        2,
    )
    all_terms = [terms] + [from_quad(terms, s) for s in range(1, nq)]
    swapped = [move(t, flip_core) for t in all_terms]

    (back_send,) = run(
        back_kernel,
        "temporal_back_projection",
        [sds(nf, 2 * nq * fr, half)],
        [geo] + all_terms + [motion_weights],
        2,
    )

    stage, block = nf // 4, half // nf
    keep_a, send_a, *parts_b = run(
        weight_kernel,
        "weight_terms",
        [sds(stage, 2, block, width)] * 2 + [sds(2, 2 * block + 8, width)] * stage,
        [geo, after(factors, back_send), factors_in, motion_weights, table, gain2]
        + all_terms
        + swapped,
        3,
        scratch=[pltpu.VMEM((2, stage, block, width), F32)] * 2,
    )

    def add(a, b, cut=False):
        outs = [sds(*a.shape[1:])] * a.shape[0] if cut else [sds(*a.shape)]
        outs = run(add_kernel, "add", outs, [a, b], 0.2)
        return outs if cut else outs[0]

    back_recv = swap(after(back_send, send_a))
    pair_a = run(
        pair_kernel,
        "add_pair",
        [sds(2, block, width)] * stage,
        [keep_a, move(send_a, flip_mid)],
        0.3,
    )
    total_a = pair_a[stage - 1]
    total_b = add(move(parts_b[stage - 1], ring), parts_b[stage - 2])
    back_recv = after(back_recv, total_a, total_b)
    backs = [back_recv] + [from_quad(back_recv, s) for s in range(1, nq)]
    for step in range(2, stage):
        last = step == stage - 1
        if last:
            total_b = after(total_b, back_recv)
            total_a = after(total_a, back_recv)
        total_a = add(move(total_a, ring), pair_a[stage - step])
        total_b = add(move(total_b, ring), parts_b[stage - 1 - step], last)
    own_b, give_b = total_b
    backs[0] = after(backs[0], total_a, give_b)
    block_output, grad_hidden = run(
        middle_kernel,
        "block_output_hidden_gradient",
        [sds(fr, pq, channels), sds(rows, channels)],
        [geo] + backs + cots + [kept, gain2],
        1.5,
        big,
    )
    total_a = add(after(move(total_a, ring), grad_hidden), pair_a[0])
    total_b = add(after(move(give_b, flip_mid), grad_hidden), own_b)
    final = []
    for g in range(nf):
        z, x, c = g // 4, (g // 2) % 2, g % 2
        for q in range(nq):
            final.append((g * nq + q, nf * q + c * (nf // 2) + x * stage + z))
    grad_hidden = after(grad_hidden, total_a, total_b)
    total_a, total_b = [lax.ppermute(t, ("frame", "quad"), final) for t in (total_a, total_b)]
    (input_grad,) = run(
        tail_kernel,
        "spatial_backward",
        [sds(fr, pq, channels)],
        [grad_hidden, activations, kept, gain1, spatial_weights],
        3.5,
        big,
    )
    everyone = nf * nq
    factor = 1.0 / math.sqrt(everyone * fr * pq)
    total_b, extra = total_b[: 2 * block], total_b[2 * block]
    weight_grad = jnp.concatenate([total_a, total_b.reshape(total_a.shape)], axis=0)
    weight_grad = weight_grad.astype(F32) * factor
    place = ((frame * nq + quad) % (nf // 2)) * block
    gain_grad = lax.dynamic_slice(extra, (place,), (block,)).astype(F32) * factor
    return block_output, input_grad, weight_grad, gain_grad


def solution(mesh):
    in_specs = (
        P("frame", "quad", None),
        P("frame", "quad", None),
        P(),
        P(),
        P(None, "quad", None),
        P(),
    )
    out_specs = (
        P("frame", "quad", None),
        P("frame", "quad", None),
        P(None, ("frame", "quad"), None),
        P(("frame", "quad")),
    )
    body = functools.partial(local, mesh.shape["quad"], mesh.shape["frame"])
    return jax.shard_map(
        body, mesh=mesh, in_specs=in_specs, out_specs=out_specs, check_vma=False
    )
```

profile of v0, /device:TPU:1, one launch (start us, length us, event | category | flops | bytes accessed | tf_op | source)
XLA Modules:
  0.0 137.1 jit_solution(7580316270490034329)
XLA Ops:
  2.5 7.3 %all-to-all-start.1 = ((bf16[16,8,640]{2,1,0:T(8,128)(2,1)}), bf16[16,8,640]{2,1,0:T(8,128)(2,1)S(1)}, u32[]{:S(2)}, u32[]{:S(2)}) async-start(bf16[16,8,640]{2,1,0:T(8,128)(2,1)} %order_cotangent.1), calls=%async_computation.1 | async-start | bytes 327680 | tf_op jit(solution)/shard_map/all_to_all | solution.py:481
  11.5 4.5 %collective-permute-done.refs_2_ = bf16[4,16,1280]{2,1,0:T(8,128)(2,1)} collective-permute-done((bf16[4,16,1280]{2,1,0:T(8,128)(2,1)}, bf16[4,16,1280]{2,1,0:T(8,128)(2,1)}, u32[]{:S(2)}, u32[]{:S(2)}) %collective-permute-start) | collective-permute-done | bytes 163872 | tf_op jit(solution)/shard_map/ppermute | solution.py:475
  17.2 2.9 %copy-done.8 = bf16[4,1280,640]{2,1,0:T(8,128)(2,1)S(1)} copy-done((bf16[4,1280,640]{2,1,0:T(8,128)(2,1)S(1)}, bf16[4,1280,640]{2,1,0:T(8,128)(2,1)}, u32[]{:S(2)}) %copy-start.8) | copy-done | bytes 6553624
  22.3 3.8 %spatial_forward.1 = (bf16[128,3200]{1,0:T(8,128)(2,1)S(1)}, bf16[16,8,640]{2,1,0:T(8,128)(2,1)S(1)}) custom-call(s32[4]{0:T(128)S(1)} %pad_add_fusion.refs_0_.quad_ref.geo, bf16[4,16,1280]{2,1,0:T(8,128)(2,1)S(1)} %copy-done.13, bf16[4,16,1280]{2,1,0:T(8,128)(2,1)} %collective-permute-done.refs_2_, f32[1280]{0:T(1024)S(1)} %copy-done.20, ...), custom_call_target="tpu_custom_call" | custom-call | flops 3000000000 | bytes 1048576 | tf_op jit(solution)/shard_map/spatial_forward/pallas_call | solution.py:430
  28.4 6.8 %all-to-all-start = ((bf16[16,8,640]{2,1,0:T(8,128)(2,1)}), bf16[16,8,640]{2,1,0:T(8,128)(2,1)S(1)}, u32[]{:S(2)}, u32[]{:S(2)}) async-start(bf16[16,8,640]{2,1,0:T(8,128)(2,1)} %copy-done.5), calls=%async_computation | async-start | bytes 327680 | tf_op jit(solution)/shard_map/all_to_all | solution.py:481
  37.2 1.9 %add_sine_fusion.pos = f32[64,1280]{1,0:T(8,128)} fusion(f32[1280]{0:T(1024)S(1)} %get-tuple-element.84, f32[1280]{0:T(1024)S(1)} %get-tuple-element.85, f32[64]{0:T(128)S(1)} %add_convert_fusion), kind=kLoop, calls=%fused_computation.1 | loop fusion | flops 163840 | bytes 338176 | tf_op jit(solution)/shard_map/sin | solution.py:458
  39.1 1.9 %collective-permute-done.2.refs_1_ = bf16[64,640]{1,0:T(8,128)(2,1)S(1)} collective-permute-done((bf16[64,640]{1,0:T(8,128)(2,1)S(1)}, bf16[64,640]{1,0:T(8,128)(2,1)S(1)}, u32[]{:S(2)}, u32[]{:S(2)}) %collective-permute-start.2) | collective-permute-done | bytes 81952 | tf_op jit(solution)/shard_map/ppermute | solution.py:478
  47.8 5.1 %collective-permute-done.4.refs_3_ = bf16[64,640]{1,0:T(8,128)(2,1)S(1)} collective-permute-done((bf16[64,640]{1,0:T(8,128)(2,1)}, bf16[64,640]{1,0:T(8,128)(2,1)S(1)}, u32[]{:S(2)}, u32[]{:S(2)}) %collective-permute-start.4) | collective-permute-done | bytes 81952 | tf_op jit(solution)/shard_map/ppermute | solution.py:478
  55.2 2.1 %collective-permute-start.7 = (bf16[64,2560]{1,0:T(8,128)(2,1)S(1)}, bf16[64,2560]{1,0:T(8,128)(2,1)S(1)}, u32[]{:S(2)}, u32[]{:S(2)}) collective-permute-start(bf16[64,2560]{1,0:T(8,128)(2,1)S(1)} %temporal_attention.1.refs_0_), channel_id=1, source_target_pairs={{0,2},{2,0},{4,6},{6,4},{8,10},{10,8},{12,14},{14,12},{16,18},{18,... | collective-permute-start | bytes 983048 | tf_op jit(solution)/shard_map/ppermute | solution.py:488
  57.3 5.1 %collective-permute-done.5.refs_1_ = bf16[64,2560]{1,0:T(8,128)(2,1)S(1)} collective-permute-done((bf16[64,2560]{1,0:T(8,128)(2,1)S(1)}, bf16[64,2560]{1,0:T(8,128)(2,1)S(1)}, u32[]{:S(2)}, u32[]{:S(2)}) %collective-permute-start.5) | collective-permute-done | bytes 327712 | tf_op jit(solution)/shard_map/ppermute | solution.py:475
  62.4 2.7 %collective-permute-start.8 = (bf16[64,2560]{1,0:T(8,128)(2,1)S(1)}, bf16[64,2560]{1,0:T(8,128)(2,1)S(1)}, u32[]{:S(2)}, u32[]{:S(2)}) collective-permute-start(bf16[64,2560]{1,0:T(8,128)(2,1)S(1)} %collective-permute-done.5.refs_1_), channel_id=1, source_target_pairs={{0,2},{2,0},{4,6},{6,4},{8,10},{10,8},{12,14},{14,12},{16,18},{18,... | collective-permute-start | bytes 983048 | tf_op jit(solution)/shard_map/ppermute | solution.py:488
  65.1 1.8 %temporal_back_projection.1 = bf16[16,16,640]{2,1,0:T(8,128)(2,1)S(1)} custom-call(s32[4]{0:T(128)S(1)} %pad_add_fusion.refs_0_.quad_ref.geo, bf16[64,2560]{1,0:T(8,128)(2,1)S(1)} %temporal_attention.1.refs_0_, bf16[64,2560]{1,0:T(8,128)(2,1)S(1)} %collective-permute-done.5.refs_1_, bf16[4,640,640]{2,1,0:T(8,128)(2,1)S(1)} %copy-done), custom_call_target="tpu_custom_call" | custom-call | flops 2000000000 | bytes 1048576 | tf_op jit(solution)/shard_map/temporal_back_projection/pallas_call | solution.py:430
  67.6 2.0 %weight_terms.1 = (bf16[4,2,40,640]{3,2,1,0:T(8,128)(2,1)S(1)}, bf16[4,2,40,640]{3,2,1,0:T(8,128)(2,1)S(1)}, bf16[2,88,640]{2,1,0:T(8,128)(2,1)S(1)}, bf16[2,88,...) custom-call(s32[4]{0:T(128)S(1)} %pad_add_fusion.refs_0_.quad_ref.geo, ...), custom_call_target="tpu_custom_call" | custom-call | flops 3000000000 | bytes 1048576 | tf_op jit(solution)/shard_map/weight_terms/pallas_call | solution.py:430
  73.3 5.6 %all-to-all-start.2 = ((bf16[16,16,640]{2,1,0:T(8,128)(2,1)}), bf16[16,16,640]{2,1,0:T(8,128)(2,1)S(1)}, u32[]{:S(2)}, u32[]{:S(2)}) async-start(bf16[16,16,640]{2,1,0:T(8,128)(2,1)} %copy-done.2), calls=%async_computation.2 | async-start | bytes 655360 | tf_op jit(solution)/shard_map/all_to_all | solution.py:481
  78.9 1.4 %collective-permute-start.9 = (bf16[4,2,40,640]{3,2,1,0:T(8,128)(2,1)}, bf16[4,2,40,640]{3,2,1,0:T(8,128)(2,1)S(1)}, u32[]{:S(2)}, u32[]{:S(2)}) collective-permute-start(bf16[4,2,40,640]{3,2,1,0:T(8,128)(2,1)} %copy-done.10), channel_id=1, source_target_pairs={{0,4},{2,6},{4,0},{6,2},{8,12},{10,14},{12,8},{14,10},{16,20},{18,... | collective-permute-start | bytes 1228808 | tf_op jit(solution)/shard_map/ppermute | solution.py:488
  81.5 11.7 %collective-permute-done.10.left = bf16[2,88,640]{2,1,0:T(8,128)(2,1)S(1)} collective-permute-done((bf16[2,88,640]{2,1,0:T(8,128)(2,1)S(1)}, bf16[2,88,640]{2,1,0:T(8,128)(2,1)S(1)}, u32[]{:S(2)}, u32[]{:S(2)}) %collective-permute-start.10) | collective-permute-done | bytes 225312 | tf_op jit(solution)/shard_map/ppermute | solution.py:488
  95.7 1.4 %collective-permute-start.11 = (bf16[2,40,640]{2,1,0:T(8,128)(2,1)S(1)}, bf16[2,40,640]{2,1,0:T(8,128)(2,1)S(1)}, u32[]{:S(2)}, u32[]{:S(2)}) collective-permute-start(bf16[2,40,640]{2,1,0:T(8,128)(2,1)S(1)} %get-tuple-element.64), channel_id=1, source_target_pairs={{0,8},{2,10},{4,12},{6,14},{8,16},{10,18},{12,20},{14,22},{16,24},... | collective-permute-start | bytes 307208 | tf_op jit(solution)/shard_map/ppermute | solution.py:488
  97.1 5.1 %collective-permute-done.13.left = bf16[2,88,640]{2,1,0:T(8,128)(2,1)S(1)} collective-permute-done((bf16[2,88,640]{2,1,0:T(8,128)(2,1)S(1)}, bf16[2,88,640]{2,1,0:T(8,128)(2,1)S(1)}, u32[]{:S(2)}, u32[]{:S(2)}) %collective-permute-start.13) | collective-permute-done | bytes 225312 | tf_op jit(solution)/shard_map/ppermute | solution.py:488
  104.6 6.9 %collective-permute-done.12.left = bf16[2,40,640]{2,1,0:T(8,128)(2,1)S(1)} collective-permute-done((bf16[2,40,640]{2,1,0:T(8,128)(2,1)S(1)}, bf16[2,40,640]{2,1,0:T(8,128)(2,1)S(1)}, u32[]{:S(2)}, u32[]{:S(2)}) %collective-permute-start.12) | collective-permute-done | bytes 102432 | tf_op jit(solution)/shard_map/ppermute | solution.py:488
  115.8 2.0 %block_output_hidden_gradient.1 = (bf16[4,16,1280]{2,1,0:T(8,128)(2,1)}, bf16[128,1280]{1,0:T(8,128)(2,1)S(1)}) custom-call(s32[4]{0:T(128)S(1)} %pad_add_fusion.refs_0_.quad_ref.geo, bf16[16,16,640]{2,1,0:T(8,128)(2,1)S(1)} %all-to-all-done.2.refs_1_, bf16[16,16,640]{2,1,0:T(8,128)(2,1)S(1)} %collective-permute-done.15.refs_2_, ...), custom_call_target="tpu_custom_call" | custom-call | flops 1500000000 | bytes 1048576 | tf_op jit(solution)/shard_map/block_output_hidden_gradient/pallas_call | solution.py:430
  117.9 4.5 %collective-permute-start.18 = (bf16[2,40,640]{2,1,0:T(8,128)(2,1)S(1)}, bf16[2,40,640]{2,1,0:T(8,128)(2,1)S(1)}, u32[]{:S(2)}, u32[]{:S(2)}) collective-permute-start(bf16[2,40,640]{2,1,0:T(8,128)(2,1)S(1)} %add.73), channel_id=1, source_target_pairs={{0,0},{1,16},{2,8},{3,24},{4,4},{5,20},{6,12},{7,28},{8,1},{9,17},... | collective-permute-start | bytes 307208 | tf_op jit(solution)/shard_map/ppermute | solution.py:623
  122.4 5.1 %collective-permute-start.19 = (bf16[88,640]{1,0:T(8,128)(2,1)S(1)}, bf16[88,640]{1,0:T(8,128)(2,1)S(1)}, u32[]{:S(2)}, u32[]{:S(2)}) collective-permute-start(bf16[88,640]{1,0:T(8,128)(2,1)S(1)} %add.74), channel_id=1, source_target_pairs={{0,0},{1,16},{2,8},{3,24},{4,4},{5,20},{6,12},{7,28},{8,1},{9,17},... | collective-permute-start | bytes 337928 | tf_op jit(solution)/shard_map/ppermute | solution.py:623
  127.6 2.9 %copy-done.9 = bf16[4,1280,640]{2,1,0:T(8,128)(2,1)S(1)} copy-done((bf16[4,1280,640]{2,1,0:T(8,128)(2,1)S(1)}, bf16[4,1280,640]{2,1,0:T(8,128)(2,1)}, u32[]{:S(2)}) %copy-start.9) | copy-done | bytes 6553624
  131.6 4.1 %spatial_backward.1 = bf16[4,16,1280]{2,1,0:T(8,128)(2,1)} custom-call(bf16[128,1280]{1,0:T(8,128)(2,1)S(1)} %get-tuple-element.83.grad_hidden, bf16[4,16,1280]{2,1,0:T(8,128)(2,1)S(1)} %copy-done.14, bf16[128,3200]{1,0:T(8,128)(2,1)S(1)} %copy-done.32, f32[1280]{0:T(1024)S(1)} %copy-done.21, bf16[4,1280,640]{2,1,0:T(8,128)(2,1)S(1)} %copy-done.9), custom_call_target="tpu_custom_call" | custom-call | flops 3500000000 | bytes 1048576 | tf_op jit(solution)/shard_map/spatial_backward/pallas_call | solution.py:430
  (117 shorter events, 37.6 us)
Async XLA Ops:
  2.5 25.3 %all-to-all-start.1 = ((bf16[16,8,640]{2,1,0:T(8,128)(2,1)}), bf16[16,8,640]{2,1,0:T(8,128)(2,1)S(1)}, u32[]{:S(2)}, u32[]{:S(2)}) async-start(bf16[16,8,640]{2,1,0:T(8,128)(2,1)} %order_cotangent.1), calls=%async_computation.1 | async-start | bytes 327680 | tf_op jit(solution)/shard_map/all_to_all | solution.py:481
  9.8 6.1 %collective-permute-start = (bf16[4,16,1280]{2,1,0:T(8,128)(2,1)}, bf16[4,16,1280]{2,1,0:T(8,128)(2,1)}, u32[]{:S(2)}, u32[]{:S(2)}) collective-permute-start(bf16[4,16,1280]{2,1,0:T(8,128)(2,1)} %xs.1), channel_id=1, source_target_pairs={{1,0},{0,1},{3,2},{2,3},{5,4},{4,5},{7,6},{6,7},{9,8},{8,9},{11,10... | collective-permute-start | bytes 491528 | tf_op jit(solution)/shard_map/ppermute | solution.py:475
  15.9 23.1 %collective-permute-start.1 = (bf16[4,16,1280]{2,1,0:T(8,128)(2,1)}, bf16[4,16,1280]{2,1,0:T(8,128)(2,1)}, u32[]{:S(2)}, u32[]{:S(2)}) collective-permute-start(bf16[4,16,1280]{2,1,0:T(8,128)(2,1)} %refs_3_.3), channel_id=1, source_target_pairs={{1,0},{0,1},{3,2},{2,3},{5,4},{4,5},{7,6},{6,7},{9,8},{8,9},{11,10... | collective-permute-start | bytes 491528 | tf_op jit(solution)/shard_map/ppermute | solution.py:475
  28.4 14.8 %all-to-all-start = ((bf16[16,8,640]{2,1,0:T(8,128)(2,1)}), bf16[16,8,640]{2,1,0:T(8,128)(2,1)S(1)}, u32[]{:S(2)}, u32[]{:S(2)}) async-start(bf16[16,8,640]{2,1,0:T(8,128)(2,1)} %copy-done.5), calls=%async_computation | async-start | bytes 327680 | tf_op jit(solution)/shard_map/all_to_all | solution.py:481
  36.9 4.1 %collective-permute-start.2 = (bf16[64,640]{1,0:T(8,128)(2,1)S(1)}, bf16[64,640]{1,0:T(8,128)(2,1)S(1)}, u32[]{:S(2)}, u32[]{:S(2)}) collective-permute-start(bf16[64,640]{1,0:T(8,128)(2,1)S(1)} %get-tuple-element.49), channel_id=1, source_target_pairs={{0,1},{1,0},{2,3},{3,2},{4,5},{5,4},{6,7},{7,6},{8,9},{9,8},{10,11... | collective-permute-start | bytes 245768 | tf_op jit(solution)/shard_map/ppermute | solution.py:478
  44.5 8.4 %collective-permute-start.3 = (bf16[64,1920]{1,0:T(8,128)(2,1)S(1)}, bf16[64,1920]{1,0:T(8,128)(2,1)S(1)}, u32[]{:S(2)}, u32[]{:S(2)}) collective-permute-start(bf16[64,1920]{1,0:T(8,128)(2,1)S(1)} %get-tuple-element.57), channel_id=1, source_target_pairs={{0,1},{1,0},{2,3},{3,2},{4,5},{5,4},{6,7},{7,6},{8,9},{9,8},{10,11... | collective-permute-start | bytes 737288 | tf_op jit(solution)/shard_map/ppermute | solution.py:478
  44.8 8.1 %collective-permute-start.4 = (bf16[64,640]{1,0:T(8,128)(2,1)}, bf16[64,640]{1,0:T(8,128)(2,1)S(1)}, u32[]{:S(2)}, u32[]{:S(2)}) collective-permute-start(bf16[64,640]{1,0:T(8,128)(2,1)} %copy-done.17), channel_id=1, source_target_pairs={{0,1},{1,0},{2,3},{3,2},{4,5},{5,4},{6,7},{7,6},{8,9},{9,8},{10,11... | collective-permute-start | bytes 245768 | tf_op jit(solution)/shard_map/ppermute | solution.py:478
  54.9 7.5 %collective-permute-start.5 = (bf16[64,2560]{1,0:T(8,128)(2,1)S(1)}, bf16[64,2560]{1,0:T(8,128)(2,1)S(1)}, u32[]{:S(2)}, u32[]{:S(2)}) collective-permute-start(bf16[64,2560]{1,0:T(8,128)(2,1)S(1)} %temporal_attention.1.refs_0_), channel_id=1, source_target_pairs={{1,0},{0,1},{3,2},{2,3},{5,4},{4,5},{7,6},{6,7},{9,8},{8,9},{11,10... | collective-permute-start | bytes 983048 | tf_op jit(solution)/shard_map/ppermute | solution.py:475
  55.2 12.4 %collective-permute-start.7 = (bf16[64,2560]{1,0:T(8,128)(2,1)S(1)}, bf16[64,2560]{1,0:T(8,128)(2,1)S(1)}, u32[]{:S(2)}, u32[]{:S(2)}) collective-permute-start(bf16[64,2560]{1,0:T(8,128)(2,1)S(1)} %temporal_attention.1.refs_0_), channel_id=1, source_target_pairs={{0,2},{2,0},{4,6},{6,4},{8,10},{10,8},{12,14},{14,12},{16,18},{18,... | collective-permute-start | bytes 983048 | tf_op jit(solution)/shard_map/ppermute | solution.py:488
  62.4 5.2 %collective-permute-start.8 = (bf16[64,2560]{1,0:T(8,128)(2,1)S(1)}, bf16[64,2560]{1,0:T(8,128)(2,1)S(1)}, u32[]{:S(2)}, u32[]{:S(2)}) collective-permute-start(bf16[64,2560]{1,0:T(8,128)(2,1)S(1)} %collective-permute-done.5.refs_1_), channel_id=1, source_target_pairs={{0,2},{2,0},{4,6},{6,4},{8,10},{10,8},{12,14},{14,12},{16,18},{18,... | collective-permute-start | bytes 983048 | tf_op jit(solution)/shard_map/ppermute | solution.py:488
  65.1 2.5 %collective-permute-start.6 = (bf16[2,128,320]{2,1,0:T(8,128)(2,1)S(1)}, bf16[2,128,320]{2,1,0:T(8,128)(2,1)S(1)}, u32[]{:S(2)}, u32[]{:S(2)}) collective-permute-start(bf16[2,128,320]{2,1,0:T(8,128)(2,1)S(1)} %get-tuple-element.60), channel_id=1, source_target_pairs={{0,2},{2,0},{4,6},{6,4},{8,10},{10,8},{12,14},{14,12},{16,18},{18,... | collective-permute-start | bytes 491528 | tf_op jit(solution)/shard_map/ppermute | solution.py:488
  73.3 54.3 %copy-start.21 = (f32[1280]{0:T(1024)S(1)}, f32[1280]{0:T(1024)}, u32[]{:S(2)}) copy-start(f32[1280]{0:T(1024)} %gain1.1) | copy-start | bytes 15364
  73.3 22.1 %all-to-all-start.2 = ((bf16[16,16,640]{2,1,0:T(8,128)(2,1)}), bf16[16,16,640]{2,1,0:T(8,128)(2,1)S(1)}, u32[]{:S(2)}, u32[]{:S(2)}) async-start(bf16[16,16,640]{2,1,0:T(8,128)(2,1)} %copy-done.2), calls=%async_computation.2 | async-start | bytes 655360 | tf_op jit(solution)/shard_map/all_to_all | solution.py:481
  78.9 15.4 %collective-permute-start.9 = (bf16[4,2,40,640]{3,2,1,0:T(8,128)(2,1)}, bf16[4,2,40,640]{3,2,1,0:T(8,128)(2,1)S(1)}, u32[]{:S(2)}, u32[]{:S(2)}) collective-permute-start(bf16[4,2,40,640]{3,2,1,0:T(8,128)(2,1)} %copy-done.10), channel_id=1, source_target_pairs={{0,4},{2,6},{4,0},{6,2},{8,12},{10,14},{12,8},{14,10},{16,20},{18,... | collective-permute-start | bytes 1228808 | tf_op jit(solution)/shard_map/ppermute | solution.py:488
  80.3 12.9 %collective-permute-start.10 = (bf16[2,88,640]{2,1,0:T(8,128)(2,1)S(1)}, bf16[2,88,640]{2,1,0:T(8,128)(2,1)S(1)}, u32[]{:S(2)}, u32[]{:S(2)}) collective-permute-start(bf16[2,88,640]{2,1,0:T(8,128)(2,1)S(1)} %get-tuple-element.65), channel_id=1, source_target_pairs={{0,8},{2,10},{4,12},{6,14},{8,16},{10,18},{12,20},{14,22},{16,24},... | collective-permute-start | bytes 675848 | tf_op jit(solution)/shard_map/ppermute | solution.py:488
  94.2 8.0 %collective-permute-start.13 = (bf16[2,88,640]{2,1,0:T(8,128)(2,1)S(1)}, bf16[2,88,640]{2,1,0:T(8,128)(2,1)S(1)}, u32[]{:S(2)}, u32[]{:S(2)}) collective-permute-start(bf16[2,88,640]{2,1,0:T(8,128)(2,1)S(1)} %add.68), channel_id=1, source_target_pairs={{0,8},{2,10},{4,12},{6,14},{8,16},{10,18},{12,20},{14,22},{16,24},... | collective-permute-start | bytes 675848 | tf_op jit(solution)/shard_map/ppermute | solution.py:488
  95.4 18.3 %collective-permute-start.15 = (bf16[16,16,640]{2,1,0:T(8,128)(2,1)S(1)}, bf16[16,16,640]{2,1,0:T(8,128)(2,1)S(1)}, u32[]{:S(2)}, u32[]{:S(2)}) collective-permute-start(bf16[16,16,640]{2,1,0:T(8,128)(2,1)S(1)} %all-to-all-done.2.refs_1_), channel_id=1, source_target_pairs={{1,0},{0,1},{3,2},{2,3},{5,4},{4,5},{7,6},{6,7},{9,8},{8,9},{11,10... | collective-permute-start | bytes 983048 | tf_op jit(solution)/shard_map/ppermute | solution.py:475
  95.7 8.7 %collective-permute-start.11 = (bf16[2,40,640]{2,1,0:T(8,128)(2,1)S(1)}, bf16[2,40,640]{2,1,0:T(8,128)(2,1)S(1)}, u32[]{:S(2)}, u32[]{:S(2)}) collective-permute-start(bf16[2,40,640]{2,1,0:T(8,128)(2,1)S(1)} %get-tuple-element.64), channel_id=1, source_target_pairs={{0,8},{2,10},{4,12},{6,14},{8,16},{10,18},{12,20},{14,22},{16,24},... | collective-permute-start | bytes 307208 | tf_op jit(solution)/shard_map/ppermute | solution.py:488
  103.2 8.3 %collective-permute-start.14 = (bf16[2,88,640]{2,1,0:T(8,128)(2,1)S(1)}, bf16[2,88,640]{2,1,0:T(8,128)(2,1)S(1)}, u32[]{:S(2)}, u32[]{:S(2)}) collective-permute-start(bf16[2,88,640]{2,1,0:T(8,128)(2,1)S(1)} %add.71), channel_id=1, source_target_pairs={{0,8},{2,10},{4,12},{6,14},{8,16},{10,18},{12,20},{14,22},{16,24},... | collective-permute-start | bytes 675848 | tf_op jit(solution)/shard_map/ppermute | solution.py:488
  104.5 7.0 %collective-permute-start.12 = (bf16[2,40,640]{2,1,0:T(8,128)(2,1)S(1)}, bf16[2,40,640]{2,1,0:T(8,128)(2,1)S(1)}, u32[]{:S(2)}, u32[]{:S(2)}) collective-permute-start(bf16[2,40,640]{2,1,0:T(8,128)(2,1)S(1)} %add.69), channel_id=1, source_target_pairs={{0,8},{2,10},{4,12},{6,14},{8,16},{10,18},{12,20},{14,22},{16,24},... | collective-permute-start | bytes 307208 | tf_op jit(solution)/shard_map/ppermute | solution.py:488
  111.5 6.4 %collective-permute-start.16 = (bf16[2,40,640]{2,1,0:T(8,128)(2,1)S(1)}, bf16[2,40,640]{2,1,0:T(8,128)(2,1)S(1)}, u32[]{:S(2)}, u32[]{:S(2)}) collective-permute-start(bf16[2,40,640]{2,1,0:T(8,128)(2,1)S(1)} %add.70), channel_id=1, source_target_pairs={{0,8},{2,10},{4,12},{6,14},{8,16},{10,18},{12,20},{14,22},{16,24},... | collective-permute-start | bytes 307208 | tf_op jit(solution)/shard_map/ppermute | solution.py:488
  112.5 9.8 %collective-permute-start.17 = (bf16[88,640]{1,0:T(8,128)(2,1)S(1)}, bf16[88,640]{1,0:T(8,128)(2,1)S(1)}, u32[]{:S(2)}, u32[]{:S(2)}) collective-permute-start(bf16[88,640]{1,0:T(8,128)(2,1)S(1)} %get-tuple-element.74), channel_id=1, source_target_pairs={{0,4},{2,6},{4,0},{6,2},{8,12},{10,14},{12,8},{14,10},{16,20},{18,... | collective-permute-start | bytes 337928 | tf_op jit(solution)/shard_map/ppermute | solution.py:488
  117.9 18.5 %collective-permute-start.18 = (bf16[2,40,640]{2,1,0:T(8,128)(2,1)S(1)}, bf16[2,40,640]{2,1,0:T(8,128)(2,1)S(1)}, u32[]{:S(2)}, u32[]{:S(2)}) collective-permute-start(bf16[2,40,640]{2,1,0:T(8,128)(2,1)S(1)} %add.73), channel_id=1, source_target_pairs={{0,0},{1,16},{2,8},{3,24},{4,4},{5,20},{6,12},{7,28},{8,1},{9,17},... | collective-permute-start | bytes 307208 | tf_op jit(solution)/shard_map/ppermute | solution.py:623
  122.4 13.3 %collective-permute-start.19 = (bf16[88,640]{1,0:T(8,128)(2,1)S(1)}, bf16[88,640]{1,0:T(8,128)(2,1)S(1)}, u32[]{:S(2)}, u32[]{:S(2)}) collective-permute-start(bf16[88,640]{1,0:T(8,128)(2,1)S(1)} %add.74), channel_id=1, source_target_pairs={{0,0},{1,16},{2,8},{3,24},{4,4},{5,20},{6,12},{7,28},{8,1},{9,17},... | collective-permute-start | bytes 337928 | tf_op jit(solution)/shard_map/ppermute | solution.py:623
  (32 other events, 146.3 us)
where the time goes:
time: 140 us; the launch traced here: 137 us
  starting transfers between devices  44.5 us (32%)
  waiting for transfers between devices  41.5 us (30%)
  local copies, waits for them, and re-layouts  27.2 us (19%)
  Pallas kernels  19.4 us (14%)
  other arithmetic  3.56 us (3%)
    unnamed x66, local copies, waits for them, and re-layouts  27.2 us
    ppermute x11, waiting for transfers between devices, move(): return lax.ppermute(x, 'frame', pairs)  24.9 us
    all_to_all x3, starting transfers between devices, swap(): return lax.all_to_all(x, 'frame', split_axis=0, concat_axis=0, tiled=True)  19.7 us
    pallas_call x19, Pallas kernels, call(): pl.pallas_call(kernel, out_shape=outs, in_specs=in_specs, out_specs=[pl.B...  19.4 us
    ppermute x11, starting transfers between devices, move(): return lax.ppermute(x, 'frame', pairs)  10.1 us
    ppermute x2, starting transfers between devices, local(): lax.ppermute(t, ('frame', 'quad'), final)  9.65 us
    ppermute x4, waiting for transfers between devices, from_quad(): return lax.ppermute(x, 'quad', [((d + s) % nq, d) for d in range(nq)])  9.6 us
    ppermute x3, waiting for transfers between devices, to_quad(): return lax.ppermute(x, 'quad', [(d, (d + s) % nq) for d in range(nq)])  6.97 us
  transfers between devices with their start and end apart: 23, of which 8 were waited for; matrix products, arithmetic and copies ran while one was open for 2% of the time, Pallas kernels for 10%

commit v1 on v0

--- a/solution.py
+++ b/solution.py
@@ -220,65 +220,46 @@
     send_out[...] = spread(dot(rows_to_sent(quad, nq, fr, pq, False), normed_two), send_out)
 
 
-def order_kernel(dims, cot, send_out):
-    nq, nf, fr, pq = dims
-    rows = flat(cot)
-    width = rows.shape[1] // nq
-    shape = (nq * fr * pq, fr * pq)
-    out, src = iota(shape, 0), iota(shape, 1)
-    want = ((out & (fr - 1)) << log2(pq)) + (out >> log2(nq * fr))
-    part = (out >> log2(fr)) & (nq - 1)
-    total = None
-    for t in range(nq):
-        pick = jnp.where((want == src) & (part == t), 1.0, 0.0).astype(BF16)
-        piece = dot(pick, rows[:, t * width : (t + 1) * width])
-        total = piece if total is None else total + piece
-    send_out[...] = spread(total, send_out)
-
-
-def split_kernel(dims, quad_ref, received, *outs):
-    nq, nf, fr, pq = dims
-    order = received_to_rows(quad_ref[0], nq, nf, fr, False)
-    rows = dot(order, flat_wide(received).astype(BF16)).astype(BF16)
+def order_kernel(dims, geo, cot, weights, send_out):
+    nq, nf, fr, pq = dims
+    order = rows_to_sent(geo[0], nq, fr, pq, False)[:, : fr * pq]
+    send_out[...] = spread(dot(order, own_lanes(flat(cot), geo[0], nq)), send_out)
+
+
+def join_kernel(dims, geo, normed, own_part, *refs):
+    nq, nf, fr, pq = dims
+    cots, send_out = refs[:-1], refs[-1]
+    order = rows_to_sent(geo[0], nq, fr, pq, False)[:, fr * pq :]
+    rows = own_lanes(jnp.concatenate([flat(c) for c in cots], axis=0), geo[0], nq)
+    total = own_part[...].astype(F32) + dot(order, rows).reshape(own_part.shape)
+    send_out[:, : nq * fr, :] = normed[...]
+    send_out[:, nq * fr :, :] = total.astype(BF16)
+
+
+def sent_part(received, i, rows):
+    part = received[:, i * rows : (i + 1) * rows, :].astype(F32)
+    return part.reshape(-1, part.shape[-1]).astype(BF16)
+
+
+def motion_kernel(dims, geo, received, weights, own_out, *sends):
+    nq, nf, fr, pq = dims
+    order = received_to_rows(geo[0], nq, nf, fr, False)
+    normed, cot = [dot(order, sent_part(received, i, nq * fr)).astype(BF16) for i in range(2)]
     tokens = nf * fr
-    for s in range(nq):
-        outs[s][...] = rows[s * tokens : (s + 1) * tokens]
-
-
-def join(refs):
-    return jnp.concatenate([ref[...] for ref in refs], axis=0)
-
-
-def cotangent_kernel(dims, *refs):
-    nq, nf, fr, pq = dims
-    weights, own_out, *sends = refs[nq:]
-    product = dot(join(refs[:nq]), weights[3])
-    tokens = nf * fr
-    own_out[...] = product[:tokens]
-    for s, send in enumerate(sends):
-        send[...] = product[(s + 1) * tokens : (s + 2) * tokens].astype(BF16)
-
-
-def motion_kernel(dims, quad_ref, received, weights, own_out, *sends):
-    nq, nf, fr, pq = dims
-    order = received_to_rows(quad_ref[0], nq, nf, fr, False)
-    rows = dot(order, flat_wide(received).astype(BF16)).astype(BF16)
-    tokens = nf * fr
-    for k in range(3):
+    for k in range(4):
         width = weights.shape[-1]
         lanes = slice(k * width, (k + 1) * width)
-        product = dot(rows, weights[k])
+        product = dot(normed if k < 3 else cot, weights[k])
         own_out[:, lanes] = product[:tokens]
         for s, send in enumerate(sends):
             send[:, lanes] = product[(s + 1) * tokens : (s + 2) * tokens].astype(BF16)
 
 
-def cut_kernel(dims, geo, received, *refs):
-    nq, nf, fr, pq = dims
-    cots, (keep, swap) = refs[:nq], refs[nq:]
+def cut_kernel(dims, geo, received, keep, swap):
+    nq, nf, fr, pq = dims
     order = received_to_rows(geo[0], nq, nf, fr, False)
-    normed = dot(order, flat_wide(received).astype(BF16))
-    for i, rows in enumerate((normed, join(cots).astype(F32))):
+    for i in range(2):
+        rows = dot(order, sent_part(received, i, nq * fr))
         half = rows.shape[1] // 2
         low, high = rows[:, :half], rows[:, half:]
         keep[i] = jnp.where(geo[1] == 0, low, high).astype(BF16)
@@ -287,18 +268,14 @@
 
 def temporal_kernel(dims, *refs):
     nq, nf, fr, pq = dims
-    qkv_own, qkv_in = refs[0], refs[1:nq]
-    grad_own, grad_in = refs[nq], refs[nq + 1 : 2 * nq]
-    out = refs[2 * nq]
+    parts, out = refs[:nq], refs[nq]
     width = HEADS * HEAD_DIM
-    total = qkv_own[...]
-    for part in qkv_in:
+    total = parts[0][...]
+    for part in parts[1:]:
         total = total + part[...].astype(F32)
-    grad = grad_own[...].astype(F32)
-    for part in grad_in:
-        grad = grad + part[...].astype(F32)
-    query, keys, values = [total[:, k * width : (k + 1) * width].astype(BF16) for k in range(3)]
-    grad = grad.astype(BF16)
+    query, keys, values, grad = [
+        total[:, k * width : (k + 1) * width].astype(BF16) for k in range(4)
+    ]
     probs = probabilities(stack_heads(query), keys, None)
     motion_out = fold_heads(dot(probs.astype(BF16), values)).astype(BF16)
     grads = attend_back(query, keys, values, grad, None, probs)
@@ -368,20 +345,6 @@
             outs_b[r][x] = rows_out.astype(BF16)
 
 
-def pair_kernel(dims, keep, moved, *outs):
-    for r, out in enumerate(outs):
-        out[...] = (keep[r].astype(F32) + moved[r].astype(F32)).astype(BF16)
-
-
-def add_kernel(dims, left, right, *outs):
-    total = (left[...].astype(F32) + right[...].astype(F32)).astype(BF16)
-    if len(outs) == 1:
-        outs[0][...] = total
-    else:
-        for i, out in enumerate(outs):
-            out[...] = total[i]
-
-
 def middle_kernel(dims, *refs):
     nq, nf, fr, pq = dims
     quad, received, cots = refs[0][0], refs[1 : 1 + nq], refs[1 + nq : 1 + 2 * nq]
@@ -392,8 +355,7 @@
     def lanes(i):
         parts = []
         for r in received:
-            rows = r[:, i * nq * fr : (i + 1) * nq * fr, :].astype(F32)
-            parts.append(dot(order, rows.reshape(nf * nq * fr, -1).astype(BF16)))
+            parts.append(dot(order, sent_part(r, i, nq * fr)))
         return place_lanes(parts, quad, nq)
 
     hidden = kept[:, 3 * HEADS * HEAD_DIM :].astype(F32)
@@ -496,13 +458,14 @@
     gain1, gain2 = spatial_gain, motion_gain
     sent = sds(nf, nq * fr, half)
     acts = [activations] + [from_quad(activations, s) for s in range(1, nq)]
-    (cot_send,) = run(order_kernel, "order_cotangent", [sent], [cotangent], 0.3)
-    cot_recv = swap(cot_send)
+    both = sds(nf, 2 * nq * fr, half)
+    (own_part,) = run(
+        order_kernel, "order_cotangent", [sent], [geo, cotangent, spatial_weights], 0.5, big
+    )
     cot_later = after(cotangent, acts[-1])
     cots = [cotangent] + [from_quad(cot_later, s) for s in range(1, nq)]
     pos = positional(frame * fr, fr, channels)
-
-    kept, send = run(
+    kept, normed = run(
         spatial_kernel,
         "spatial_forward",
         [sds(rows, 3 * width + channels), sent],
@@ -510,87 +473,56 @@
         3,
         big,
     )
+    (send,) = run(join_kernel, "join_sent", [both], [geo, normed, own_part] + cots[1:], 0.5)
     received = swap(send)
-
-    cot_parts = run(
-        split_kernel,
-        "split_cotangent",
-        [sds(tokens, half)] * nq,
-        [geo, after(cot_recv, send)],
-        0.3,
-    )
-    cot_parts = [cot_parts[0]] + [to_quad(cot_parts[nq - s], nq - s) for s in range(1, nq)]
-    grad_parts = run(
-        cotangent_kernel,
-        "cotangent_projection",
-        [sds(tokens, width, dtype=F32)] + [sds(tokens, width)] * (nq - 1),
-        [after(cot_parts[0], cots[-1])] + cot_parts[1:] + [motion_weights],
-        0.4,
-    )
-    grad_own = grad_parts[0]
-    table = positional(after(frame * 0, cot_parts[0]), tokens, channels)
-    grad_parts = [grad_own] + [to_quad(p, s + 1) for s, p in enumerate(grad_parts[1:])]
-
-    qkv_parts = run(
+    table = positional(after(frame * 0, send), tokens, channels)
+
+    parts = run(
         motion_kernel,
         "motion_projection",
-        [sds(tokens, 3 * width, dtype=F32)] + [sds(tokens, 3 * width)] * (nq - 1),
-        [geo, after(received, grad_own, table), motion_weights],
-        0.8,
+        [sds(tokens, 4 * width, dtype=F32)] + [sds(tokens, 4 * width)] * (nq - 1),
+        [geo, after(received, table), motion_weights],
+        1.5,
     )
     factors, factors_out = run(
         cut_kernel,
         "cut_factors",
         [sds(2, rows, half // 2)] * 2,
-        [geo, after(received, qkv_parts[0])] + cot_parts,
+        [geo, after(received, parts[0])],
         0.5,
     )
-    qkv_parts = [qkv_parts[0]] + [to_quad(part, s + 1) for s, part in enumerate(qkv_parts[1:])]
     factors_in = move(factors_out, flip_core)
-
-    (terms,) = run(
-        temporal_kernel,
-        "temporal_attention",
-        [sds(tokens, 4 * width)],
-        [after(qkv_parts[0], factors)] + qkv_parts[1:] + grad_parts,
-        2,
-    )
+    parts = [after(parts[0], factors_in)] + [to_quad(p, s + 1) for s, p in enumerate(parts[1:])]
+
+    (terms,) = run(temporal_kernel, "temporal_attention", [sds(tokens, 4 * width)], parts, 2)
     all_terms = [terms] + [from_quad(terms, s) for s in range(1, nq)]
     swapped = [move(t, flip_core) for t in all_terms]
-
-    (back_send,) = run(
-        back_kernel,
-        "temporal_back_projection",
-        [sds(nf, 2 * nq * fr, half)],
-        [geo] + all_terms + [motion_weights],
-        2,
-    )
 
     stage, block = nf // 4, half // nf
     keep_a, send_a, *parts_b = run(
         weight_kernel,
         "weight_terms",
         [sds(stage, 2, block, width)] * 2 + [sds(2, 2 * block + 8, width)] * stage,
-        [geo, after(factors, back_send), factors_in, motion_weights, table, gain2]
+        [geo, factors, factors_in, motion_weights, table, gain2]
         + all_terms
         + swapped,
         3,
         scratch=[pltpu.VMEM((2, stage, block, width), F32)] * 2,
     )
 
-    def add(a, b, cut=False):
-        outs = [sds(*a.shape[1:])] * a.shape[0] if cut else [sds(*a.shape)]
-        outs = run(add_kernel, "add", outs, [a, b], 0.2)
-        return outs if cut else outs[0]
-
-    back_recv = swap(after(back_send, send_a))
-    pair_a = run(
-        pair_kernel,
-        "add_pair",
-        [sds(2, block, width)] * stage,
-        [keep_a, move(send_a, flip_mid)],
-        0.3,
-    )
+    (back_send,) = run(
+        back_kernel,
+        "temporal_back_projection",
+        [sds(nf, 2 * nq * fr, half)],
+        [geo, after(all_terms[0], send_a)] + all_terms[1:] + [motion_weights],
+        2,
+    )
+
+    def add(a, b):
+        return (a.astype(F32) + b.astype(F32)).astype(BF16)
+
+    back_recv = swap(back_send)
+    pair_a = add(keep_a, move(send_a, flip_mid))
     total_a = pair_a[stage - 1]
     total_b = add(move(parts_b[stage - 1], ring), parts_b[stage - 2])
     back_recv = after(back_recv, total_a, total_b)
@@ -601,8 +533,8 @@
             total_b = after(total_b, back_recv)
             total_a = after(total_a, back_recv)
         total_a = add(move(total_a, ring), pair_a[stage - step])
-        total_b = add(move(total_b, ring), parts_b[stage - 1 - step], last)
-    own_b, give_b = total_b
+        total_b = add(move(total_b, ring), parts_b[stage - 1 - step])
+    own_b, give_b = total_b[0], total_b[1]
     backs[0] = after(backs[0], total_a, give_b)
     block_output, grad_hidden = run(
         middle_kernel,

time: 140 us -> 125 us (0.89); the launches traced: 137 us -> 124 us
  local copies, waits for them, and re-layouts: 27.2 us -> 15.5 us
  starting transfers between devices: 44.5 us -> 37.4 us
  waiting for transfers between devices: 41.5 us -> 46.7 us
    unnamed x66 -> x28, local copies, waits for them, and re-layouts: 27.2 us -> 15.4 us
    all_to_all x3 -> x2, waiting for transfers between devices: 0.01 us -> 9.65 us  [swap(): return lax.all_to_all(x, 'frame', split_axis=0, concat_axis=0, tiled=True)]
    all_to_all x3 -> x2, starting transfers between devices: 19.7 us -> 10.8 us  [swap(): return lax.all_to_all(x, 'frame', split_axis=0, concat_axis=0, tiled=True)]
    ppermute x4, waiting for transfers between devices: 9.6 us -> 6.23 us  [from_quad(): return lax.ppermute(x, 'quad', [((d + s) % nq, d) for d in range(nq)])]
    ppermute x2, starting transfers between devices: 9.65 us -> 11.7 us  [local(): lax.ppermute(t, ('frame', 'quad'), final)]
    ppermute x3 -> x1, starting transfers between devices: 1.85 us -> 0.29 us  [to_quad(): return lax.ppermute(x, 'quad', [(d, (d + s) % nq) for d in range(nq)])]
    ppermute x11, starting transfers between devices: 10.1 us -> 11.5 us  [move(): return lax.ppermute(x, 'frame', pairs)]
    ppermute x3 -> x1, waiting for transfers between devices: 6.97 us -> 5.87 us  [to_quad(): return lax.ppermute(x, 'quad', [(d, (d + s) % nq) for d in range(nq)])]
  transfers between devices with their start and end apart: 23 -> 20, of which waited for: 8 -> 10; matrix products, arithmetic and copies ran while one was open for 2% -> 3% of each run, Pallas kernels for 10% -> 11%
where the time goes in v1:
time: 125 us; the launch traced here: 124 us
  waiting for transfers between devices  46.7 us (37%)
  starting transfers between devices  37.4 us (30%)
  Pallas kernels  19.4 us (16%)
  local copies, waits for them, and re-layouts  15.5 us (12%)
  other arithmetic  4.23 us (3%)
    ppermute x11, waiting for transfers between devices, move(): return lax.ppermute(x, 'frame', pairs)  24.9 us
    pallas_call x10, Pallas kernels, call(): pl.pallas_call(kernel, out_shape=outs, in_specs=in_specs, out_specs=[pl.B...  19.4 us
    unnamed x28, local copies, waits for them, and re-layouts  15.4 us
    ppermute x2, starting transfers between devices, local(): lax.ppermute(t, ('frame', 'quad'), final)  11.7 us
    ppermute x11, starting transfers between devices, move(): return lax.ppermute(x, 'frame', pairs)  11.5 us
    all_to_all x2, starting transfers between devices, swap(): return lax.all_to_all(x, 'frame', split_axis=0, concat_axis=0, tiled=True)  10.8 us
    all_to_all x2, waiting for transfers between devices, swap(): return lax.all_to_all(x, 'frame', split_axis=0, concat_axis=0, tiled=True)  9.65 us
    ppermute x4, waiting for transfers between devices, from_quad(): return lax.ppermute(x, 'quad', [((d + s) % nq, d) for d in range(nq)])  6.23 us
  transfers between devices with their start and end apart: 20, of which 10 were waited for; matrix products, arithmetic and copies ran while one was open for 3% of the time, Pallas kernels for 11%

profile of v1, /device:TPU:1, one launch (start us, length us, event | category | flops | bytes accessed | tf_op | source)
XLA Modules:
  0.0 124.1 jit_solution(1167748853303332146)
XLA Ops:
  0.7 2.1 %collective-permute-start = (bf16[4,16,1280]{2,1,0:T(8,128)(2,1)}, bf16[4,16,1280]{2,1,0:T(8,128)(2,1)S(1)}, u32[]{:S(2)}, u32[]{:S(2)}) collective-permute-start(bf16[4,16,1280]{2,1,0:T(8,128)(2,1)} %xs.1), channel_id=1, source_target_pairs={{1,0},{0,1},{3,2},{2,3},{5,4},{4,5},{7,6},{6,7},{9,8},{8,9},{11,10... | collective-permute-start | bytes 491528 | tf_op jit(solution)/shard_map/ppermute | solution.py:437
  3.1 2.9 %copy-done = bf16[4,1280,640]{2,1,0:T(8,128)(2,1)S(1)} copy-done((bf16[4,1280,640]{2,1,0:T(8,128)(2,1)S(1)}, bf16[4,1280,640]{2,1,0:T(8,128)(2,1)}, u32[]{:S(2)}) %copy-start) | copy-done | bytes 6553624
  8.1 1.7 %copy-done.1 = bf16[4,1280,640]{2,1,0:T(8,128)(2,1)S(1)} copy-done((bf16[4,1280,640]{2,1,0:T(8,128)(2,1)S(1)}, bf16[4,1280,640]{2,1,0:T(8,128)(2,1)}, u32[]{:S(2)}) %copy-start.1) | copy-done | bytes 6553624
  9.8 3.4 %spatial_forward.1 = (bf16[128,3200]{1,0:T(8,128)(2,1)S(1)}, bf16[16,8,640]{2,1,0:T(8,128)(2,1)S(1)}) custom-call(s32[4]{0:T(128)S(1)} %pad_add_fusion.refs_0_.geo.quad_ref, bf16[4,16,1280]{2,1,0:T(8,128)(2,1)S(1)} %copy-done.8, bf16[4,16,1280]{2,1,0:T(8,128)(2,1)S(1)} %collective-permute-done.refs_2_, f32[1280]{0:T(1024)S(1)} %copy-done.10, ...), custom_call_target="tpu_custom_call" | custom-call | flops 3000000000 | bytes 1048576 | tf_op jit(solution)/shard_map/spatial_forward/pallas_call | solution.py:392
  15.7 6.8 %all-to-all-start = ((bf16[16,16,640]{2,1,0:T(8,128)(2,1)}), bf16[16,16,640]{2,1,0:T(8,128)(2,1)S(1)}, u32[]{:S(2)}, u32[]{:S(2)}) async-start(bf16[16,16,640]{2,1,0:T(8,128)(2,1)} %join_sent.1), calls=%async_computation | async-start | bytes 655360 | tf_op jit(solution)/shard_map/all_to_all | solution.py:443
  23.6 9.7 %all-to-all-done.received = bf16[16,16,640]{2,1,0:T(8,128)(2,1)S(1)} async-done(((bf16[16,16,640]{2,1,0:T(8,128)(2,1)}), bf16[16,16,640]{2,1,0:T(8,128)(2,1)S(1)}, u32[]{:S(2)}, u32[]{:S(2)}) %all-to-all-start) | async-done | bytes 327712 | tf_op jit(solution)/shard_map/all_to_all | solution.py:443
  33.3 1.9 %copy-done.5 = bf16[4,640,640]{2,1,0:T(8,128)(2,1)S(1)} copy-done((bf16[4,640,640]{2,1,0:T(8,128)(2,1)S(1)}, bf16[4,640,640]{2,1,0:T(8,128)(2,1)}, u32[]{:S(2)}) %copy-start.5) | copy-done | bytes 3276824
  39.7 5.9 %collective-permute-done.3.refs_1_ = bf16[64,2560]{1,0:T(8,128)(2,1)S(1)} collective-permute-done((bf16[64,2560]{1,0:T(8,128)(2,1)S(1)}, bf16[64,2560]{1,0:T(8,128)(2,1)S(1)}, u32[]{:S(2)}, u32[]{:S(2)}) %collective-permute-start.3) | collective-permute-done | bytes 327712 | tf_op jit(solution)/shard_map/ppermute | solution.py:440
  48.5 6.2 %collective-permute-done.4.refs_1_ = bf16[64,2560]{1,0:T(8,128)(2,1)S(1)} collective-permute-done((bf16[64,2560]{1,0:T(8,128)(2,1)S(1)}, bf16[64,2560]{1,0:T(8,128)(2,1)S(1)}, u32[]{:S(2)}, u32[]{:S(2)}) %collective-permute-start.4) | collective-permute-done | bytes 327712 | tf_op jit(solution)/shard_map/ppermute | solution.py:437
  54.7 2.2 %collective-permute-start.6 = (bf16[64,2560]{1,0:T(8,128)(2,1)S(1)}, bf16[64,2560]{1,0:T(8,128)(2,1)S(1)}, u32[]{:S(2)}, u32[]{:S(2)}) collective-permute-start(bf16[64,2560]{1,0:T(8,128)(2,1)S(1)} %collective-permute-done.4.refs_1_), channel_id=1, source_target_pairs={{0,2},{2,0},{4,6},{6,4},{8,10},{10,8},{12,14},{14,12},{16,18},{18,... | collective-permute-start | bytes 983048 | tf_op jit(solution)/shard_map/ppermute | solution.py:450
  58.2 2.0 %weight_terms.1 = (bf16[4,2,40,640]{3,2,1,0:T(8,128)(2,1)S(1)}, bf16[4,2,40,640]{3,2,1,0:T(8,128)(2,1)S(1)}, bf16[2,88,640]{2,1,0:T(8,128)(2,1)S(1)}, bf16[2,88,...) custom-call(s32[4]{0:T(128)S(1)} %pad_add_fusion.refs_0_.geo.quad_ref, ...), custom_call_target="tpu_custom_call" | custom-call | flops 3000000000 | bytes 1048576 | tf_op jit(solution)/shard_map/weight_terms/pallas_call | solution.py:392
  61.4 1.9 %copy-done.7 = bf16[4,640,640]{2,1,0:T(8,128)(2,1)S(1)} copy-done((bf16[4,640,640]{2,1,0:T(8,128)(2,1)S(1)}, bf16[4,640,640]{2,1,0:T(8,128)(2,1)}, u32[]{:S(2)}) %copy-start.7) | copy-done | bytes 3276824
  63.3 2.5 %temporal_back_projection.1 = bf16[16,16,640]{2,1,0:T(8,128)(2,1)} custom-call(s32[4]{0:T(128)S(1)} %pad_add_fusion.refs_0_.geo.quad_ref, bf16[64,2560]{1,0:T(8,128)(2,1)S(1)} %temporal_attention.1.refs_0_, bf16[64,2560]{1,0:T(8,128)(2,1)S(1)} %collective-permute-done.4.refs_1_, bf16[4,640,640]{2,1,0:T(8,128)(2,1)S(1)} %copy-done.7), custom_call_target="tpu_custom_call" | custom-call | flops 2000000000 | bytes 1048576 | tf_op jit(solution)/shard_map/temporal_back_projection/pallas_call | solution.py:392
  65.8 4.0 %all-to-all-start.1 = ((bf16[16,16,640]{2,1,0:T(8,128)(2,1)}), bf16[16,16,640]{2,1,0:T(8,128)(2,1)S(1)}, u32[]{:S(2)}, u32[]{:S(2)}) async-start(bf16[16,16,640]{2,1,0:T(8,128)(2,1)} %temporal_back_projection.1), calls=%async_computation.1 | async-start | bytes 655360 | tf_op jit(solution)/shard_map/all_to_all | solution.py:443
  73.6 10.6 %collective-permute-done.8 = bf16[2,88,640]{2,1,0:T(8,128)(2,1)S(1)} collective-permute-done((bf16[2,88,640]{2,1,0:T(8,128)(2,1)S(1)}, bf16[2,88,640]{2,1,0:T(8,128)(2,1)S(1)}, u32[]{:S(2)}, u32[]{:S(2)}) %collective-permute-start.8) | collective-permute-done | bytes 225312 | tf_op jit(solution)/shard_map/ppermute | solution.py:450
  84.3 2.1 %collective-permute-done.9 = bf16[2,40,640]{2,1,0:T(8,128)(2,1)S(1)} collective-permute-done((bf16[2,40,640]{2,1,0:T(8,128)(2,1)S(1)}, bf16[2,40,640]{2,1,0:T(8,128)(2,1)S(1)}, u32[]{:S(2)}, u32[]{:S(2)}) %collective-permute-start.9) | collective-permute-done | bytes 102432 | tf_op jit(solution)/shard_map/ppermute | solution.py:450
  86.4 1.9 %collective-permute-start.10 = (bf16[2,40,640]{2,1,0:T(8,128)(2,1)S(1)}, bf16[2,40,640]{2,1,0:T(8,128)(2,1)S(1)}, u32[]{:S(2)}, u32[]{:S(2)}) collective-permute-start(bf16[2,40,640]{2,1,0:T(8,128)(2,1)S(1)} %fusion.3), channel_id=1, source_target_pairs={{0,8},{2,10},{4,12},{6,14},{8,16},{10,18},{12,20},{14,22},{16,24},... | collective-permute-start | bytes 307208 | tf_op jit(solution)/shard_map/ppermute | solution.py:450
  88.3 3.4 %collective-permute-done.11 = bf16[2,88,640]{2,1,0:T(8,128)(2,1)S(1)} collective-permute-done((bf16[2,88,640]{2,1,0:T(8,128)(2,1)S(1)}, bf16[2,88,640]{2,1,0:T(8,128)(2,1)S(1)}, u32[]{:S(2)}, u32[]{:S(2)}) %collective-permute-start.11) | collective-permute-done | bytes 225312 | tf_op jit(solution)/shard_map/ppermute | solution.py:450
  92.1 1.8 %collective-permute-done.10 = bf16[2,40,640]{2,1,0:T(8,128)(2,1)S(1)} collective-permute-done((bf16[2,40,640]{2,1,0:T(8,128)(2,1)S(1)}, bf16[2,40,640]{2,1,0:T(8,128)(2,1)S(1)}, u32[]{:S(2)}, u32[]{:S(2)}) %collective-permute-start.10) | collective-permute-done | bytes 102432 | tf_op jit(solution)/shard_map/ppermute | solution.py:450
  94.0 4.7 %collective-permute-done.12 = bf16[2,88,640]{2,1,0:T(8,128)(2,1)S(1)} collective-permute-done((bf16[2,88,640]{2,1,0:T(8,128)(2,1)S(1)}, bf16[2,88,640]{2,1,0:T(8,128)(2,1)S(1)}, u32[]{:S(2)}, u32[]{:S(2)}) %collective-permute-start.12) | collective-permute-done | bytes 225312 | tf_op jit(solution)/shard_map/ppermute | solution.py:450
  102.9 4.8 %collective-permute-start.16 = (bf16[2,40,640]{2,1,0:T(8,128)(2,1)S(1)}, bf16[2,40,640]{2,1,0:T(8,128)(2,1)S(1)}, u32[]{:S(2)}, u32[]{:S(2)}) collective-permute-start(bf16[2,40,640]{2,1,0:T(8,128)(2,1)S(1)} %fusion.1), channel_id=1, source_target_pairs={{0,0},{1,16},{2,8},{3,24},{4,4},{5,20},{6,12},{7,28},{8,1},{9,17},... | collective-permute-start | bytes 307208 | tf_op jit(solution)/shard_map/ppermute | solution.py:555
  107.7 6.9 %collective-permute-start.17 = (bf16[88,640]{1,0:T(8,128)(2,1)S(1)}, bf16[88,640]{1,0:T(8,128)(2,1)S(1)}, u32[]{:S(2)}, u32[]{:S(2)}) collective-permute-start(bf16[88,640]{1,0:T(8,128)(2,1)S(1)} %fusion), channel_id=1, source_target_pairs={{0,0},{1,16},{2,8},{3,24},{4,4},{5,20},{6,12},{7,28},{8,1},{9,17},... | collective-permute-start | bytes 337928 | tf_op jit(solution)/shard_map/ppermute | solution.py:555
  114.6 2.9 %copy-done.2 = bf16[4,1280,640]{2,1,0:T(8,128)(2,1)S(1)} copy-done((bf16[4,1280,640]{2,1,0:T(8,128)(2,1)S(1)}, bf16[4,1280,640]{2,1,0:T(8,128)(2,1)}, u32[]{:S(2)}) %copy-start.2) | copy-done | bytes 6553624
  118.6 4.1 %spatial_backward.1 = bf16[4,16,1280]{2,1,0:T(8,128)(2,1)} custom-call(bf16[128,1280]{1,0:T(8,128)(2,1)S(1)} %get-tuple-element.57.grad_hidden, bf16[4,16,1280]{2,1,0:T(8,128)(2,1)S(1)} %copy-done.8, bf16[128,3200]{1,0:T(8,128)(2,1)S(1)} %copy-done.13, f32[1280]{0:T(1024)S(1)} %copy-done.10, bf16[4,1280,640]{2,1,0:T(8,128)(2,1)S(1)} %copy-done.2), custom_call_target="tpu_custom_call" | custom-call | flops 3500000000 | bytes 1048576 | tf_op jit(solution)/shard_map/spatial_backward/pallas_call | solution.py:392
  (74 shorter events, 27.0 us)
Async XLA Ops:
  0.6 7.4 %copy-start.9 = (f32[1280]{0:T(1024)S(1)}, f32[1280]{0:T(1024)}, u32[]{:S(2)}) copy-start(f32[1280]{0:T(1024)} %refs_6_.3) | copy-start | bytes 15364
  0.6 7.4 %copy-start.10 = (f32[1280]{0:T(1024)S(1)}, f32[1280]{0:T(1024)}, u32[]{:S(2)}) copy-start(f32[1280]{0:T(1024)} %gain1.1) | copy-start | bytes 15364
  0.7 7.0 %collective-permute-start = (bf16[4,16,1280]{2,1,0:T(8,128)(2,1)}, bf16[4,16,1280]{2,1,0:T(8,128)(2,1)S(1)}, u32[]{:S(2)}, u32[]{:S(2)}) collective-permute-start(bf16[4,16,1280]{2,1,0:T(8,128)(2,1)} %xs.1), channel_id=1, source_target_pairs={{1,0},{0,1},{3,2},{2,3},{5,4},{4,5},{7,6},{6,7},{9,8},{8,9},{11,10... | collective-permute-start | bytes 491528 | tf_op jit(solution)/shard_map/ppermute | solution.py:437
  7.7 6.5 %collective-permute-start.1 = (bf16[4,16,1280]{2,1,0:T(8,128)(2,1)S(1)}, bf16[4,16,1280]{2,1,0:T(8,128)(2,1)S(1)}, u32[]{:S(2)}, u32[]{:S(2)}) collective-permute-start(bf16[4,16,1280]{2,1,0:T(8,128)(2,1)S(1)} %copy-done.3), channel_id=1, source_target_pairs={{1,0},{0,1},{3,2},{2,3},{5,4},{4,5},{7,6},{6,7},{9,8},{8,9},{11,10... | collective-permute-start | bytes 491528 | tf_op jit(solution)/shard_map/ppermute | solution.py:437
  15.7 17.6 %all-to-all-start = ((bf16[16,16,640]{2,1,0:T(8,128)(2,1)}), bf16[16,16,640]{2,1,0:T(8,128)(2,1)S(1)}, u32[]{:S(2)}, u32[]{:S(2)}) async-start(bf16[16,16,640]{2,1,0:T(8,128)(2,1)} %join_sent.1), calls=%async_computation | async-start | bytes 655360 | tf_op jit(solution)/shard_map/all_to_all | solution.py:443
  35.2 23.0 %copy-start.6 = (bf16[4,640,640]{2,1,0:T(8,128)(2,1)S(1)}, bf16[4,640,640]{2,1,0:T(8,128)(2,1)}, u32[]{:S(2)}) copy-start(bf16[4,640,640]{2,1,0:T(8,128)(2,1)} %refs_2_.1) | copy-start | bytes 9830404
  36.6 9.0 %collective-permute-start.3 = (bf16[64,2560]{1,0:T(8,128)(2,1)S(1)}, bf16[64,2560]{1,0:T(8,128)(2,1)S(1)}, u32[]{:S(2)}, u32[]{:S(2)}) collective-permute-start(bf16[64,2560]{1,0:T(8,128)(2,1)S(1)} %get-tuple-element.39), channel_id=1, source_target_pairs={{0,1},{1,0},{2,3},{3,2},{4,5},{5,4},{6,7},{7,6},{8,9},{9,8},{10,11... | collective-permute-start | bytes 983048 | tf_op jit(solution)/shard_map/ppermute | solution.py:440
  37.9 1.8 %collective-permute-start.2 = (bf16[2,128,320]{2,1,0:T(8,128)(2,1)S(1)}, bf16[2,128,320]{2,1,0:T(8,128)(2,1)S(1)}, u32[]{:S(2)}, u32[]{:S(2)}) collective-permute-start(bf16[2,128,320]{2,1,0:T(8,128)(2,1)S(1)} %get-tuple-element.37), channel_id=1, source_target_pairs={{0,2},{2,0},{4,6},{6,4},{8,10},{10,8},{12,14},{14,12},{16,18},{18,... | collective-permute-start | bytes 491528 | tf_op jit(solution)/shard_map/ppermute | solution.py:450
  46.7 8.0 %collective-permute-start.4 = (bf16[64,2560]{1,0:T(8,128)(2,1)S(1)}, bf16[64,2560]{1,0:T(8,128)(2,1)S(1)}, u32[]{:S(2)}, u32[]{:S(2)}) collective-permute-start(bf16[64,2560]{1,0:T(8,128)(2,1)S(1)} %temporal_attention.1.refs_0_), channel_id=1, source_target_pairs={{1,0},{0,1},{3,2},{2,3},{5,4},{4,5},{7,6},{6,7},{9,8},{8,9},{11,10... | collective-permute-start | bytes 983048 | tf_op jit(solution)/shard_map/ppermute | solution.py:437
  47.0 9.9 %collective-permute-start.5 = (bf16[64,2560]{1,0:T(8,128)(2,1)S(1)}, bf16[64,2560]{1,0:T(8,128)(2,1)S(1)}, u32[]{:S(2)}, u32[]{:S(2)}) collective-permute-start(bf16[64,2560]{1,0:T(8,128)(2,1)S(1)} %temporal_attention.1.refs_0_), channel_id=1, source_target_pairs={{0,2},{2,0},{4,6},{6,4},{8,10},{10,8},{12,14},{14,12},{16,18},{18,... | collective-permute-start | bytes 983048 | tf_op jit(solution)/shard_map/ppermute | solution.py:450
  54.7 3.4 %collective-permute-start.6 = (bf16[64,2560]{1,0:T(8,128)(2,1)S(1)}, bf16[64,2560]{1,0:T(8,128)(2,1)S(1)}, u32[]{:S(2)}, u32[]{:S(2)}) collective-permute-start(bf16[64,2560]{1,0:T(8,128)(2,1)S(1)} %collective-permute-done.4.refs_1_), channel_id=1, source_target_pairs={{0,2},{2,0},{4,6},{6,4},{8,10},{10,8},{12,14},{14,12},{16,18},{18,... | collective-permute-start | bytes 983048 | tf_op jit(solution)/shard_map/ppermute | solution.py:450
  60.2 39.8 %copy-start.4 = (bf16[4,16,1280]{2,1,0:T(8,128)(2,1)S(1)}, bf16[4,16,1280]{2,1,0:T(8,128)(2,1)}, u32[]{:S(2)}) copy-start(bf16[4,16,1280]{2,1,0:T(8,128)(2,1)} %refs_3_.3) | copy-start | bytes 491524
  60.2 11.0 %collective-permute-start.7 = (bf16[4,2,40,640]{3,2,1,0:T(8,128)(2,1)S(1)}, bf16[4,2,40,640]{3,2,1,0:T(8,128)(2,1)}, u32[]{:S(2)}, u32[]{:S(2)}) collective-permute-start(bf16[4,2,40,640]{3,2,1,0:T(8,128)(2,1)S(1)} %get-tuple-element.41), channel_id=1, source_target_pairs={{0,4},{2,6},{4,0},{6,2},{8,12},{10,14},{12,8},{14,10},{16,20},{18,... | collective-permute-start | bytes 1228808 | tf_op jit(solution)/shard_map/ppermute | solution.py:450
  65.8 20.6 %all-to-all-start.1 = ((bf16[16,16,640]{2,1,0:T(8,128)(2,1)}), bf16[16,16,640]{2,1,0:T(8,128)(2,1)S(1)}, u32[]{:S(2)}, u32[]{:S(2)}) async-start(bf16[16,16,640]{2,1,0:T(8,128)(2,1)} %temporal_back_projection.1), calls=%async_computation.1 | async-start | bytes 655360 | tf_op jit(solution)/shard_map/all_to_all | solution.py:443
  69.8 14.4 %collective-permute-start.8 = (bf16[2,88,640]{2,1,0:T(8,128)(2,1)S(1)}, bf16[2,88,640]{2,1,0:T(8,128)(2,1)S(1)}, u32[]{:S(2)}, u32[]{:S(2)}) collective-permute-start(bf16[2,88,640]{2,1,0:T(8,128)(2,1)S(1)} %get-tuple-element.44), channel_id=1, source_target_pairs={{0,8},{2,10},{4,12},{6,14},{8,16},{10,18},{12,20},{14,22},{16,24},... | collective-permute-start | bytes 675848 | tf_op jit(solution)/shard_map/ppermute | solution.py:450
  72.3 14.0 %collective-permute-start.9 = (bf16[2,40,640]{2,1,0:T(8,128)(2,1)S(1)}, bf16[2,40,640]{2,1,0:T(8,128)(2,1)S(1)}, u32[]{:S(2)}, u32[]{:S(2)}) collective-permute-start(bf16[2,40,640]{2,1,0:T(8,128)(2,1)S(1)} %slice_bitcast_fusion.5), channel_id=1, source_target_pairs={{0,8},{2,10},{4,12},{6,14},{8,16},{10,18},{12,20},{14,22},{16,24},... | collective-permute-start | bytes 307208 | tf_op jit(solution)/shard_map/ppermute | solution.py:450
  84.2 7.5 %collective-permute-start.11 = (bf16[2,88,640]{2,1,0:T(8,128)(2,1)S(1)}, bf16[2,88,640]{2,1,0:T(8,128)(2,1)S(1)}, u32[]{:S(2)}, u32[]{:S(2)}) collective-permute-start(bf16[2,88,640]{2,1,0:T(8,128)(2,1)S(1)} %add_convert_fusion.3), channel_id=1, source_target_pairs={{0,8},{2,10},{4,12},{6,14},{8,16},{10,18},{12,20},{14,22},{16,24},... | collective-permute-start | bytes 675848 | tf_op jit(solution)/shard_map/ppermute | solution.py:450
  86.4 7.5 %collective-permute-start.10 = (bf16[2,40,640]{2,1,0:T(8,128)(2,1)S(1)}, bf16[2,40,640]{2,1,0:T(8,128)(2,1)S(1)}, u32[]{:S(2)}, u32[]{:S(2)}) collective-permute-start(bf16[2,40,640]{2,1,0:T(8,128)(2,1)S(1)} %fusion.3), channel_id=1, source_target_pairs={{0,8},{2,10},{4,12},{6,14},{8,16},{10,18},{12,20},{14,22},{16,24},... | collective-permute-start | bytes 307208 | tf_op jit(solution)/shard_map/ppermute | solution.py:450
  91.8 8.2 %collective-permute-start.13 = (bf16[16,16,640]{2,1,0:T(8,128)(2,1)S(1)}, bf16[16,16,640]{2,1,0:T(8,128)(2,1)S(1)}, u32[]{:S(2)}, u32[]{:S(2)}) collective-permute-start(bf16[16,16,640]{2,1,0:T(8,128)(2,1)S(1)} %all-to-all-done.1.refs_1_), channel_id=1, source_target_pairs={{1,0},{0,1},{3,2},{2,3},{5,4},{4,5},{7,6},{6,7},{9,8},{8,9},{11,10... | collective-permute-start | bytes 983048 | tf_op jit(solution)/shard_map/ppermute | solution.py:437
  92.1 6.6 %collective-permute-start.12 = (bf16[2,88,640]{2,1,0:T(8,128)(2,1)S(1)}, bf16[2,88,640]{2,1,0:T(8,128)(2,1)S(1)}, u32[]{:S(2)}, u32[]{:S(2)}) collective-permute-start(bf16[2,88,640]{2,1,0:T(8,128)(2,1)S(1)} %add_convert_fusion.2), channel_id=1, source_target_pairs={{0,8},{2,10},{4,12},{6,14},{8,16},{10,18},{12,20},{14,22},{16,24},... | collective-permute-start | bytes 675848 | tf_op jit(solution)/shard_map/ppermute | solution.py:450
  94.0 8.9 %collective-permute-start.14 = (bf16[2,40,640]{2,1,0:T(8,128)(2,1)S(1)}, bf16[2,40,640]{2,1,0:T(8,128)(2,1)S(1)}, u32[]{:S(2)}, u32[]{:S(2)}) collective-permute-start(bf16[2,40,640]{2,1,0:T(8,128)(2,1)S(1)} %fusion.2), channel_id=1, source_target_pairs={{0,8},{2,10},{4,12},{6,14},{8,16},{10,18},{12,20},{14,22},{16,24},... | collective-permute-start | bytes 307208 | tf_op jit(solution)/shard_map/ppermute | solution.py:450
  98.8 8.9 %collective-permute-start.15 = (bf16[88,640]{1,0:T(8,128)(2,1)S(1)}, bf16[88,640]{1,0:T(8,128)(2,1)S(1)}, u32[]{:S(2)}, u32[]{:S(2)}) collective-permute-start(bf16[88,640]{1,0:T(8,128)(2,1)S(1)} %slice_bitcast_fusion.1), channel_id=1, source_target_pairs={{0,4},{2,6},{4,0},{6,2},{8,12},{10,14},{12,8},{14,10},{16,20},{18,... | collective-permute-start | bytes 337928 | tf_op jit(solution)/shard_map/ppermute | solution.py:450
  102.9 20.5 %collective-permute-start.16 = (bf16[2,40,640]{2,1,0:T(8,128)(2,1)S(1)}, bf16[2,40,640]{2,1,0:T(8,128)(2,1)S(1)}, u32[]{:S(2)}, u32[]{:S(2)}) collective-permute-start(bf16[2,40,640]{2,1,0:T(8,128)(2,1)S(1)} %fusion.1), channel_id=1, source_target_pairs={{0,0},{1,16},{2,8},{3,24},{4,4},{5,20},{6,12},{7,28},{8,1},{9,17},... | collective-permute-start | bytes 307208 | tf_op jit(solution)/shard_map/ppermute | solution.py:555
  107.7 15.0 %collective-permute-start.17 = (bf16[88,640]{1,0:T(8,128)(2,1)S(1)}, bf16[88,640]{1,0:T(8,128)(2,1)S(1)}, u32[]{:S(2)}, u32[]{:S(2)}) collective-permute-start(bf16[88,640]{1,0:T(8,128)(2,1)S(1)} %fusion), channel_id=1, source_target_pairs={{0,0},{1,16},{2,8},{3,24},{4,4},{5,20},{6,12},{7,28},{8,1},{9,17},... | collective-permute-start | bytes 337928 | tf_op jit(solution)/shard_map/ppermute | solution.py:555
  (10 other events, 19.4 us)
